TPU v7x, 512 devices: a whole 4x8x8 slice. The times are simulated.
512 devices in a mesh: blk: 32 (over y_lo, z), dp: 16 (over y_hi, x, core).
Axes of the slice: x: 4, y: 8 (y_hi: 2, y_lo: 4; y = y_hi * 4 + y_lo), z: 8, core: 2. Of those that a mesh axis runs over, the one named last changes fastest.
Arguments:
- image_embed: bfloat16 [131072, 1152], P(('blk', 'dp')), may hold values from -0.29882812 to 0.29882812
- text_embed: bfloat16 [131072, 1152], P(('blk', 'dp')), may hold values from -0.29882812 to 0.29882812
- log_temp: float32 [1], replicated, may hold values from 1.1 to 2.3
- bias: float32 [1], replicated, may hold values from -4 to -1
Outputs:
- loss: float32 [1], replicated
- grad_logt: float32 [1], replicated
- grad_bias: float32 [1], replicated
- grad_image: float32 [131072, 1152], P(('blk', 'dp'))
- grad_text: float32 [131072, 1152], P(('blk', 'dp'))
All inputs are finite; a program needn't handle non-finite values.
Results may differ from a plain program's by a relative error of at most 0.0033.
The roundings to bfloat16 on the way count: a program that leaves them out, or rounds other values in their place, can miss the bound.
Values may be sent and summed in bfloat16 or wider, within the bound.
No kernel may reach another device: no remote copies, remote signals or barrier semaphores. Data moves between devices by JAX's collectives and lax.ppermute only.
A program may use at most 64 MiB of HBM per device.

v0:
```python
import jax
import jax.numpy as jnp
from jax import lax
from jax.sharding import PartitionSpec as P


def shifted(array, axis, by):
    length = lax.axis_size(axis)
    return lax.ppermute(array, axis, [(i, (i + by) % length) for i in range(length)])


def normalize(x):
    xf = x.astype(jnp.float32)
    inv = lax.rsqrt(jnp.sum(xf * xf, axis=-1, keepdims=True) + 1e-06)
    return (xf * inv, inv)


def denormalize(grad, unit, inv):
    return inv * (grad - unit * jnp.sum(unit * grad, axis=-1, keepdims=True))


def score_tile(img_n, other, temp, shift_b, offset):
    dots = lax.dot_general(
        img_n, other, (((1,), (1,)), ((), ())), preferred_element_type=jnp.float32
    )
    logit = temp * dots + shift_b
    if offset == 0:
        sign = 2.0 * jnp.eye(dots.shape[0], dtype=jnp.float32) - 1.0
    else:
        sign = -jnp.ones_like(dots)
    part_loss = -jnp.sum(jax.nn.log_sigmoid(sign * logit))
    dl = -sign * jax.nn.sigmoid(-sign * logit)
    part_temp = jnp.sum(dl * temp * dots)
    part_bias = jnp.sum(dl)
    g = (temp * dl).astype(jnp.bfloat16)
    img_part = jnp.dot(g, other, preferred_element_type=jnp.float32)
    txt_part = lax.dot_general(
        g, img_n, (((0,), (0,)), ((), ())), preferred_element_type=jnp.float32
    )
    return (jnp.stack([part_loss, part_temp, part_bias]), img_part, txt_part)


def body(image_embed, text_embed, log_temp, bias):
    unit_i, inv_i = normalize(image_embed)
    unit_t, inv_t = normalize(text_embed)
    img_n = unit_i.astype(jnp.bfloat16)
    txt_n = unit_t.astype(jnp.bfloat16)
    temp = jnp.exp(log_temp[0])
    shift_b = bias[0]
    blocks = lax.axis_size("blk")
    rounds = min(8, blocks // 2)
    half_band = rounds // 2
    pair_count = img_n.shape[0] * blocks * lax.axis_size("dp")
    totals = jnp.zeros((3,), jnp.float32)
    gimg = jnp.zeros(unit_i.shape, jnp.float32)
    other = shifted(txt_n, "blk", half_band)
    carried = jnp.zeros(unit_t.shape, jnp.float32)
    for step in range(rounds):
        parts, img_part, txt_part = score_tile(img_n, other, temp, shift_b, step - half_band)
        totals = totals + lax.psum(parts, ("blk", "dp"))
        gimg = gimg + img_part
        carried = carried + txt_part
        if step + 1 < rounds:
            other = shifted(other, "blk", -1)
            carried = shifted(carried, "blk", -1)
    gtxt = shifted(carried, "blk", half_band - 1)
    totals = totals / pair_count
    grad_image = denormalize(gimg, unit_i, inv_i)
    grad_text = denormalize(gtxt, unit_t, inv_t)
    return (totals[0:1], totals[1:2], totals[2:3], grad_image, grad_text)


def solution(mesh):
    placed = (P(("blk", "dp"), None), P(("blk", "dp"), None), P(), P())
    return jax.shard_map(
        body,
        mesh=mesh,
        in_specs=placed,
        out_specs=(P(), P(), P(), P(("blk", "dp"), None), P(("blk", "dp"), None)),
        check_vma=False,
    )
```

profile of v0, /device:TPU:1, one launch (start us, length us, event | category | flops | bytes accessed | tf_op | source)
XLA Modules:
  0.0 542.2 jit_solution(11529334279617116662)
XLA Ops:
  0.6 1.3 fusion.13
  3.2 11.5 %collective-permute-start = (bf16[256,1152]{1,0:T(8,128)(2,1)S(1)}, bf16[256,1152]{1,0:T(8,128)(2,1)S(1)}, u32[]{:S(2)}, u32[]{:S(2)}) collective-permute-start(bf16[256,1152]{1,0:T(8,128)(2,1)S(1)} %fusion.2), channel_id=1, source_target_pairs={{0,64},{16,80},{32,96},{48,112},{64,128},{80,144},{96,160},{112,17... | collective-permute-start | bytes 1769480 | tf_op jit(solution)/shard_map/ppermute | solution.py:9
  16.2 20.5 %collective-permute-done = bf16[256,1152]{1,0:T(8,128)(2,1)S(1)} collective-permute-done((bf16[256,1152]{1,0:T(8,128)(2,1)S(1)}, bf16[256,1152]{1,0:T(8,128)(2,1)S(1)}, u32[]{:S(2)}, u32[]{:S(2)}) %collective-permute-start) | collective-permute-done | bytes 589856 | tf_op jit(solution)/shard_map/ppermute | solution.py:9
  38.4 12.0 %collective-permute-start.8 = (f32[256,1152]{1,0:T(8,128)S(1)}, f32[256,1152]{1,0:T(8,128)S(1)}, u32[]{:S(2)}, u32[]{:S(2)}) collective-permute-start(f32[256,1152]{1,0:T(8,128)S(1)} %fusion.22), channel_id=1, source_target_pairs={{0,496},{16,0},{32,16},{48,32},{64,48},{80,64},{96,80},{112,96},{1... | collective-permute-start | bytes 3538952 | tf_op jit(solution)/shard_map/ppermute | solution.py:9
  50.4 4.2 collective-permute-start.1
  54.6 32.7 %collective-permute-done.1 = bf16[256,1152]{1,0:T(8,128)(2,1)S(1)} collective-permute-done((bf16[256,1152]{1,0:T(8,128)(2,1)S(1)}, bf16[256,1152]{1,0:T(8,128)(2,1)S(1)}, u32[]{:S(2)}, u32[]{:S(2)}) %collective-permute-start.1) | collective-permute-done | bytes 589856 | tf_op jit(solution)/shard_map/ppermute | solution.py:9
  89.0 8.0 %collective-permute-start.9 = (f32[256,1152]{1,0:T(8,128)S(1)}, f32[256,1152]{1,0:T(8,128)S(1)}, u32[]{:S(2)}, u32[]{:S(2)}) collective-permute-start(f32[256,1152]{1,0:T(8,128)S(1)} %convolution_add_fusion), channel_id=1, source_target_pairs={{0,496},{16,0},{32,16},{48,32},{64,48},{80,64},{96,80},{112,96},{1... | collective-permute-start | bytes 3538952 | tf_op jit(solution)/shard_map/ppermute | solution.py:9
  97.0 1.9 collective-permute-start.2
  98.9 34.0 %collective-permute-done.2 = bf16[256,1152]{1,0:T(8,128)(2,1)S(1)} collective-permute-done((bf16[256,1152]{1,0:T(8,128)(2,1)S(1)}, bf16[256,1152]{1,0:T(8,128)(2,1)S(1)}, u32[]{:S(2)}, u32[]{:S(2)}) %collective-permute-start.2) | collective-permute-done | bytes 589856 | tf_op jit(solution)/shard_map/ppermute | solution.py:9
  134.7 8.0 %collective-permute-start.10 = (f32[256,1152]{1,0:T(8,128)S(1)}, f32[256,1152]{1,0:T(8,128)S(1)}, u32[]{:S(2)}, u32[]{:S(2)}) collective-permute-start(f32[256,1152]{1,0:T(8,128)S(1)} %add.222), channel_id=1, source_target_pairs={{0,496},{16,0},{32,16},{48,32},{64,48},{80,64},{96,80},{112,96},{1... | collective-permute-start | bytes 3538952 | tf_op jit(solution)/shard_map/ppermute | solution.py:9
  142.7 1.9 collective-permute-start.3
  144.6 33.1 %collective-permute-done.3 = bf16[256,1152]{1,0:T(8,128)(2,1)S(1)} collective-permute-done((bf16[256,1152]{1,0:T(8,128)(2,1)S(1)}, bf16[256,1152]{1,0:T(8,128)(2,1)S(1)}, u32[]{:S(2)}, u32[]{:S(2)}) %collective-permute-start.3) | collective-permute-done | bytes 589856 | tf_op jit(solution)/shard_map/ppermute | solution.py:9
  179.5 8.0 %collective-permute-start.11 = (f32[256,1152]{1,0:T(8,128)S(1)}, f32[256,1152]{1,0:T(8,128)S(1)}, u32[]{:S(2)}, u32[]{:S(2)}) collective-permute-start(f32[256,1152]{1,0:T(8,128)S(1)} %add.223), channel_id=1, source_target_pairs={{0,496},{16,0},{32,16},{48,32},{64,48},{80,64},{96,80},{112,96},{1... | collective-permute-start | bytes 3538952 | tf_op jit(solution)/shard_map/ppermute | solution.py:9
  187.5 1.9 collective-permute-start.4
  189.5 32.1 %collective-permute-done.4 = bf16[256,1152]{1,0:T(8,128)(2,1)S(1)} collective-permute-done((bf16[256,1152]{1,0:T(8,128)(2,1)S(1)}, bf16[256,1152]{1,0:T(8,128)(2,1)S(1)}, u32[]{:S(2)}, u32[]{:S(2)}) %collective-permute-start.4) | collective-permute-done | bytes 589856 | tf_op jit(solution)/shard_map/ppermute | solution.py:9
  221.6 1.3 fusion.18
  223.5 8.0 %collective-permute-start.12 = (f32[256,1152]{1,0:T(8,128)S(1)}, f32[256,1152]{1,0:T(8,128)S(1)}, u32[]{:S(2)}, u32[]{:S(2)}) collective-permute-start(f32[256,1152]{1,0:T(8,128)S(1)} %add.224), channel_id=1, source_target_pairs={{0,496},{16,0},{32,16},{48,32},{64,48},{80,64},{96,80},{112,96},{1... | collective-permute-start | bytes 3538952 | tf_op jit(solution)/shard_map/ppermute | solution.py:9
  231.5 1.9 collective-permute-start.5
  234.2 30.5 %collective-permute-done.5 = bf16[256,1152]{1,0:T(8,128)(2,1)S(1)} collective-permute-done((bf16[256,1152]{1,0:T(8,128)(2,1)S(1)}, bf16[256,1152]{1,0:T(8,128)(2,1)S(1)}, u32[]{:S(2)}, u32[]{:S(2)}) %collective-permute-start.5) | collective-permute-done | bytes 589856 | tf_op jit(solution)/shard_map/ppermute | solution.py:9
  266.5 8.0 %collective-permute-start.13 = (f32[256,1152]{1,0:T(8,128)S(1)}, f32[256,1152]{1,0:T(8,128)S(1)}, u32[]{:S(2)}, u32[]{:S(2)}) collective-permute-start(f32[256,1152]{1,0:T(8,128)S(1)} %add.225), channel_id=1, source_target_pairs={{0,496},{16,0},{32,16},{48,32},{64,48},{80,64},{96,80},{112,96},{1... | collective-permute-start | bytes 3538952 | tf_op jit(solution)/shard_map/ppermute | solution.py:9
  274.9 1.9 collective-permute-start.6
  277.5 29.2 %collective-permute-done.6 = bf16[256,1152]{1,0:T(8,128)(2,1)S(1)} collective-permute-done((bf16[256,1152]{1,0:T(8,128)(2,1)S(1)}, bf16[256,1152]{1,0:T(8,128)(2,1)S(1)}, u32[]{:S(2)}, u32[]{:S(2)}) %collective-permute-start.6) | collective-permute-done | bytes 589856 | tf_op jit(solution)/shard_map/ppermute | solution.py:9
  306.7 8.0 %collective-permute-start.7 = (bf16[256,1152]{1,0:T(8,128)(2,1)S(1)}, bf16[256,1152]{1,0:T(8,128)(2,1)S(1)}, u32[]{:S(2)}, u32[]{:S(2)}) collective-permute-start(bf16[256,1152]{1,0:T(8,128)(2,1)S(1)} %collective-permute-done.6), channel_id=1, source_target_pairs={{0,496},{16,0},{32,16},{48,32},{64,48},{80,64},{96,80},{112,96},{1... | collective-permute-start | bytes 1769480 | tf_op jit(solution)/shard_map/ppermute | solution.py:9
  316.5 2.1 collective-permute-start.14
  319.0 2.6 collective-permute-done.7
  321.5 1.8 fusion.21
  323.3 15.1 %maximum_add_fusion.2 = f32[3]{0:T(128)S(1)} fusion(f32[1]{0:T(128)} %bitcast.25, f32[1]{0:T(128)} %bitcast.24, f32[1]{0:T(128)} %bitcast.23, f32[1]{0:T(128)} %bitcast.22, f32[1]{0:T(128)} %bitcast.21, f32[1]{0:T(128)} %bitcast.20, f32[1]{0:T(128)} %bitcast.19, f32[1]{0:T(128)} %bitcast.18, f32[1]{0:T(128)} %bitcast.17, f32[1]{0:T(128)} %bitcast.16, ...), kind=kLoop, calls=%fused_computation.92 | loop fusion | flops 69 | bytes 108 | tf_op jit(solution)/shard_map/add | solution.py:60
  338.8 113.2 %psum.70 = f32[3]{0:T(128)S(1)} all-reduce(f32[3]{0:T(128)S(1)} %maximum_add_fusion.2), channel_id=1, replica_groups=mesh['blk'=32,'dp'=16] {'blk','dp'}, use_global_device_ids=true, to_apply=%region_5.6 | all-reduce | flops 3 | bytes 24 | tf_op jit(solution)/shard_map/psum | solution.py:60
  452.0 1.4 fusion.29
  453.4 1.4 add.227
  454.9 2.9 collective-permute-start.15
  460.2 80.4 %collective-permute-done.15 = f32[256,1152]{1,0:T(8,128)S(1)} collective-permute-done((f32[256,1152]{1,0:T(8,128)S(1)}, f32[256,1152]{1,0:T(8,128)S(1)}, u32[]{:S(2)}, u32[]{:S(2)}) %collective-permute-start.15) | collective-permute-done | bytes 1179680 | tf_op jit(solution)/shard_map/ppermute | solution.py:9
  (48 shorter events, 18.9 us)
Async XLA Ops:
  0.6 15.4 %copy-start.1 = (bf16[256,1152]{1,0:T(8,128)(2,1)S(1)}, bf16[256,1152]{1,0:T(8,128)(2,1)}, u32[]{:S(2)}) copy-start(bf16[256,1152]{1,0:T(8,128)(2,1)} %param.4) | copy-start | bytes 1769476
  3.2 33.5 %collective-permute-start = (bf16[256,1152]{1,0:T(8,128)(2,1)S(1)}, bf16[256,1152]{1,0:T(8,128)(2,1)S(1)}, u32[]{:S(2)}, u32[]{:S(2)}) collective-permute-start(bf16[256,1152]{1,0:T(8,128)(2,1)S(1)} %fusion.2), channel_id=1, source_target_pairs={{0,64},{16,80},{32,96},{48,112},{64,128},{80,144},{96,160},{112,17... | collective-permute-start | bytes 1769480 | tf_op jit(solution)/shard_map/ppermute | solution.py:9
  38.4 50.1 %collective-permute-start.8 = (f32[256,1152]{1,0:T(8,128)S(1)}, f32[256,1152]{1,0:T(8,128)S(1)}, u32[]{:S(2)}, u32[]{:S(2)}) collective-permute-start(f32[256,1152]{1,0:T(8,128)S(1)} %fusion.22), channel_id=1, source_target_pairs={{0,496},{16,0},{32,16},{48,32},{64,48},{80,64},{96,80},{112,96},{1... | collective-permute-start | bytes 3538952 | tf_op jit(solution)/shard_map/ppermute | solution.py:9
  50.4 36.8 %collective-permute-start.1 = (bf16[256,1152]{1,0:T(8,128)(2,1)S(1)}, bf16[256,1152]{1,0:T(8,128)(2,1)S(1)}, u32[]{:S(2)}, u32[]{:S(2)}) collective-permute-start(bf16[256,1152]{1,0:T(8,128)(2,1)S(1)} %collective-permute-done), channel_id=1, source_target_pairs={{0,496},{16,0},{32,16},{48,32},{64,48},{80,64},{96,80},{112,96},{1... | collective-permute-start | bytes 1769480 | tf_op jit(solution)/shard_map/ppermute | solution.py:9
  89.0 45.6 %collective-permute-start.9 = (f32[256,1152]{1,0:T(8,128)S(1)}, f32[256,1152]{1,0:T(8,128)S(1)}, u32[]{:S(2)}, u32[]{:S(2)}) collective-permute-start(f32[256,1152]{1,0:T(8,128)S(1)} %convolution_add_fusion), channel_id=1, source_target_pairs={{0,496},{16,0},{32,16},{48,32},{64,48},{80,64},{96,80},{112,96},{1... | collective-permute-start | bytes 3538952 | tf_op jit(solution)/shard_map/ppermute | solution.py:9
  97.0 35.9 %collective-permute-start.2 = (bf16[256,1152]{1,0:T(8,128)(2,1)S(1)}, bf16[256,1152]{1,0:T(8,128)(2,1)S(1)}, u32[]{:S(2)}, u32[]{:S(2)}) collective-permute-start(bf16[256,1152]{1,0:T(8,128)(2,1)S(1)} %collective-permute-done.1), channel_id=1, source_target_pairs={{0,496},{16,0},{32,16},{48,32},{64,48},{80,64},{96,80},{112,96},{1... | collective-permute-start | bytes 1769480 | tf_op jit(solution)/shard_map/ppermute | solution.py:9
  134.7 44.7 %collective-permute-start.10 = (f32[256,1152]{1,0:T(8,128)S(1)}, f32[256,1152]{1,0:T(8,128)S(1)}, u32[]{:S(2)}, u32[]{:S(2)}) collective-permute-start(f32[256,1152]{1,0:T(8,128)S(1)} %add.222), channel_id=1, source_target_pairs={{0,496},{16,0},{32,16},{48,32},{64,48},{80,64},{96,80},{112,96},{1... | collective-permute-start | bytes 3538952 | tf_op jit(solution)/shard_map/ppermute | solution.py:9
  142.7 35.0 %collective-permute-start.3 = (bf16[256,1152]{1,0:T(8,128)(2,1)S(1)}, bf16[256,1152]{1,0:T(8,128)(2,1)S(1)}, u32[]{:S(2)}, u32[]{:S(2)}) collective-permute-start(bf16[256,1152]{1,0:T(8,128)(2,1)S(1)} %collective-permute-done.2), channel_id=1, source_target_pairs={{0,496},{16,0},{32,16},{48,32},{64,48},{80,64},{96,80},{112,96},{1... | collective-permute-start | bytes 1769480 | tf_op jit(solution)/shard_map/ppermute | solution.py:9
  179.5 43.8 %collective-permute-start.11 = (f32[256,1152]{1,0:T(8,128)S(1)}, f32[256,1152]{1,0:T(8,128)S(1)}, u32[]{:S(2)}, u32[]{:S(2)}) collective-permute-start(f32[256,1152]{1,0:T(8,128)S(1)} %add.223), channel_id=1, source_target_pairs={{0,496},{16,0},{32,16},{48,32},{64,48},{80,64},{96,80},{112,96},{1... | collective-permute-start | bytes 3538952 | tf_op jit(solution)/shard_map/ppermute | solution.py:9
  187.5 34.1 %collective-permute-start.4 = (bf16[256,1152]{1,0:T(8,128)(2,1)S(1)}, bf16[256,1152]{1,0:T(8,128)(2,1)S(1)}, u32[]{:S(2)}, u32[]{:S(2)}) collective-permute-start(bf16[256,1152]{1,0:T(8,128)(2,1)S(1)} %collective-permute-done.3), channel_id=1, source_target_pairs={{0,496},{16,0},{32,16},{48,32},{64,48},{80,64},{96,80},{112,96},{1... | collective-permute-start | bytes 1769480 | tf_op jit(solution)/shard_map/ppermute | solution.py:9
  223.5 42.8 %collective-permute-start.12 = (f32[256,1152]{1,0:T(8,128)S(1)}, f32[256,1152]{1,0:T(8,128)S(1)}, u32[]{:S(2)}, u32[]{:S(2)}) collective-permute-start(f32[256,1152]{1,0:T(8,128)S(1)} %add.224), channel_id=1, source_target_pairs={{0,496},{16,0},{32,16},{48,32},{64,48},{80,64},{96,80},{112,96},{1... | collective-permute-start | bytes 3538952 | tf_op jit(solution)/shard_map/ppermute | solution.py:9
  231.5 33.1 %collective-permute-start.5 = (bf16[256,1152]{1,0:T(8,128)(2,1)S(1)}, bf16[256,1152]{1,0:T(8,128)(2,1)S(1)}, u32[]{:S(2)}, u32[]{:S(2)}) collective-permute-start(bf16[256,1152]{1,0:T(8,128)(2,1)S(1)} %collective-permute-done.4), channel_id=1, source_target_pairs={{0,496},{16,0},{32,16},{48,32},{64,48},{80,64},{96,80},{112,96},{1... | collective-permute-start | bytes 1769480 | tf_op jit(solution)/shard_map/ppermute | solution.py:9
  266.5 49.9 %collective-permute-start.13 = (f32[256,1152]{1,0:T(8,128)S(1)}, f32[256,1152]{1,0:T(8,128)S(1)}, u32[]{:S(2)}, u32[]{:S(2)}) collective-permute-start(f32[256,1152]{1,0:T(8,128)S(1)} %add.225), channel_id=1, source_target_pairs={{0,496},{16,0},{32,16},{48,32},{64,48},{80,64},{96,80},{112,96},{1... | collective-permute-start | bytes 3538952 | tf_op jit(solution)/shard_map/ppermute | solution.py:9
  274.9 31.8 %collective-permute-start.6 = (bf16[256,1152]{1,0:T(8,128)(2,1)S(1)}, bf16[256,1152]{1,0:T(8,128)(2,1)S(1)}, u32[]{:S(2)}, u32[]{:S(2)}) collective-permute-start(bf16[256,1152]{1,0:T(8,128)(2,1)S(1)} %collective-permute-done.5), channel_id=1, source_target_pairs={{0,496},{16,0},{32,16},{48,32},{64,48},{80,64},{96,80},{112,96},{1... | collective-permute-start | bytes 1769480 | tf_op jit(solution)/shard_map/ppermute | solution.py:9
  306.7 14.8 %collective-permute-start.7 = (bf16[256,1152]{1,0:T(8,128)(2,1)S(1)}, bf16[256,1152]{1,0:T(8,128)(2,1)S(1)}, u32[]{:S(2)}, u32[]{:S(2)}) collective-permute-start(bf16[256,1152]{1,0:T(8,128)(2,1)S(1)} %collective-permute-done.6), channel_id=1, source_target_pairs={{0,496},{16,0},{32,16},{48,32},{64,48},{80,64},{96,80},{112,96},{1... | collective-permute-start | bytes 1769480 | tf_op jit(solution)/shard_map/ppermute | solution.py:9
  316.5 137.0 %collective-permute-start.14 = (f32[256,1152]{1,0:T(8,128)S(1)}, f32[256,1152]{1,0:T(8,128)}, u32[]{:S(2)}, u32[]{:S(2)}) collective-permute-start(f32[256,1152]{1,0:T(8,128)S(1)} %add.226), channel_id=1, source_target_pairs={{0,496},{16,0},{32,16},{48,32},{64,48},{80,64},{96,80},{112,96},{1... | collective-permute-start | bytes 3538952 | tf_op jit(solution)/shard_map/ppermute | solution.py:9
  453.4 5.0 copy-start.2
  454.9 85.7 %collective-permute-start.15 = (f32[256,1152]{1,0:T(8,128)S(1)}, f32[256,1152]{1,0:T(8,128)S(1)}, u32[]{:S(2)}, u32[]{:S(2)}) collective-permute-start(f32[256,1152]{1,0:T(8,128)S(1)} %add.227), channel_id=1, source_target_pairs={{0,48},{16,64},{32,80},{48,96},{64,112},{80,128},{96,144},{112,160... | collective-permute-start | bytes 3538952 | tf_op jit(solution)/shard_map/ppermute | solution.py:9
  458.9 81.7 %copy-start = (bf16[256,1152]{1,0:T(8,128)(2,1)S(1)}, bf16[256,1152]{1,0:T(8,128)(2,1)}, u32[]{:S(2)}) copy-start(bf16[256,1152]{1,0:T(8,128)(2,1)} %param.5) | copy-start | bytes 1769476
where the time goes:
time: 549 us; the launch traced here: 542 us
  waiting for transfers between devices  295 us (54%)
  blocking collectives  113 us (21%)
  starting transfers between devices  90.4 us (16%)
  other arithmetic  22.8 us (4%)
  matrix products  17.9 us (3%)
    ppermute x16, waiting for transfers between devices, shifted(): lax.ppermute(array, axis, [(i, (i + by) % length) for i in range(length)])  295 us
    psum x1, blocking collectives, body(): totals = totals + lax.psum(parts, ('blk', 'dp'))  113 us
    ppermute x16, starting transfers between devices, shifted(): lax.ppermute(array, axis, [(i, (i + by) % length) for i in range(length)])  90.4 us
    add x1, other arithmetic, body(): totals = totals + lax.psum(parts, ('blk', 'dp'))  15.1 us
  transfers between devices with their start and end apart: 16, of which 9 were waited for; matrix products, arithmetic and copies ran while one was open for 6% of the time, Pallas kernels for 0%

commit v1 on v0

v1 whole, which is shorter than its diff:
```python
import functools

import jax
import jax.numpy as jnp
from jax import lax
from jax.experimental import pallas as pl
from jax.experimental.pallas import tpu as pltpu
from jax.sharding import PartitionSpec as P

F32, BF16 = jnp.float32, jnp.bfloat16


def shifted(array, by):
    length = lax.axis_size("blk")
    return lax.ppermute(array, "blk", [(i, (i + by) % length) for i in range(length)])


def normal(raw):
    xf = raw.astype(F32)
    inv = lax.rsqrt(jnp.sum(xf * xf, axis=-1, keepdims=True) + 1e-06)
    return xf * inv, inv


def products(a, b):
    return lax.dot_general(a, b, (((1,), (1,)), ((), ())), preferred_element_type=F32)


def sigmoid(x):
    return 1.0 / (1.0 + jnp.exp(-x))


def fold(v):
    r = jnp.sum(v.reshape(v.shape[0] // 8, 8, v.shape[1]), axis=0)
    return sum(r[:, i : i + 128] for i in range(0, v.shape[1], 128))


def add_terms(sums_ref, u, dl, scaled):
    sums_ref[0:8, :] += fold(jnp.maximum(u, 0.0) + jnp.log1p(jnp.exp(-jnp.abs(u))))
    sums_ref[8:16, :] += fold(dl * scaled)
    sums_ref[16:24, :] += fold(dl)


def off_diagonal(own, other, temp, bias, sums_ref=None):
    scaled = temp * products(own, other)
    logit = scaled + bias
    dl = sigmoid(logit)
    if sums_ref is not None:
        add_terms(sums_ref, logit, dl, scaled)
    return (temp * dl).astype(BF16)


def own_kernel(temp_ref, bias_ref, img_ref, txt_ref, img_n_ref, txt_n_ref, gimg_ref, gtxt_ref, sums_ref):
    temp, bias = jnp.exp(temp_ref[...]), bias_ref[...]
    img_n_ref[...] = normal(img_ref[...])[0].astype(BF16)
    txt_n_ref[...] = normal(txt_ref[...])[0].astype(BF16)
    scaled = temp * products(img_n_ref[...], txt_n_ref[...])
    logit = scaled + bias
    rows = lax.broadcasted_iota(jnp.int32, logit.shape, 0)
    cols = lax.broadcasted_iota(jnp.int32, logit.shape, 1)
    diagonal = rows == cols
    u = jnp.where(diagonal, -logit, logit)
    s = sigmoid(u)
    dl = jnp.where(diagonal, -s, s)
    sums_ref[...] = jnp.zeros_like(sums_ref)
    add_terms(sums_ref, u, dl, scaled)
    g = (temp * dl).astype(BF16)
    gimg_ref[...] = jnp.dot(g, txt_n_ref[...], preferred_element_type=F32)
    gtxt_ref[...] = lax.dot_general(
        g, img_n_ref[...], (((0,), (0,)), ((), ())), preferred_element_type=F32
    )


def own_tile(temp, bias, image, text):
    block = image.shape
    return pl.pallas_call(
        own_kernel,
        out_shape=(
            jax.ShapeDtypeStruct(block, BF16),
            jax.ShapeDtypeStruct(block, BF16),
            jax.ShapeDtypeStruct(block, F32),
            jax.ShapeDtypeStruct(block, F32),
            jax.ShapeDtypeStruct((24, 128), F32),
        ),
        compiler_params=pltpu.CompilerParams(vmem_limit_bytes=24 << 20),
        name="own_tile",
    )(temp, bias, image, text)


def pair_kernel(with_older, counted, keep, *refs):
    refs = list(refs)
    temp_ref, bias_ref, img_n_ref, txt_n_ref, t_ref, i_ref, gimg_in, gtxt_in = refs[:8]
    del refs[:8]
    temp, bias = jnp.exp(temp_ref[...]), bias_ref[...]
    older = None
    sums_in = None
    if with_older:
        older = refs.pop(0)
    if counted:
        sums_in = refs.pop(0)
    gimg_ref, gtxt_ref = refs[:2]
    del refs[:2]
    sums_ref = None
    if counted:
        sums_ref = refs.pop(0)
        sums_ref[...] = sums_in[...]
    t_n = normal(t_ref[...])[0].astype(BF16)
    i_n = normal(i_ref[...])[0].astype(BF16)
    if keep:
        refs.pop(0)[...] = i_n
    g = off_diagonal(img_n_ref[...], t_n, temp, bias, sums_ref)
    gimg_ref[...] = gimg_in[...] + jnp.dot(g, t_n, preferred_element_type=F32)
    g = off_diagonal(txt_n_ref[...], i_n, temp, bias)
    gtxt_ref[...] = gtxt_in[...] + jnp.dot(g, i_n, preferred_element_type=F32)
    if older is not None:
        off_diagonal(older[...], t_n, temp, bias, sums_ref)


def pair(temp, bias, own, t, i, acc, sums=None, older=None, keep=False):
    block = t.shape
    args = [temp, bias, *own, t, i, *acc]
    outs = [jax.ShapeDtypeStruct(block, F32)] * 2
    aliases = {6: 0, 7: 1}
    if older is not None:
        args.append(older)
    if sums is not None:
        aliases[len(args)] = len(outs)
        args.append(sums)
        outs.append(jax.ShapeDtypeStruct((24, 128), F32))
    if keep:
        outs.append(jax.ShapeDtypeStruct(block, BF16))
    return pl.pallas_call(
        functools.partial(pair_kernel, older is not None, sums is not None, keep),
        out_shape=tuple(outs),
        input_output_aliases=aliases,
        compiler_params=pltpu.CompilerParams(vmem_limit_bytes=24 << 20),
        name="pair",
    )(*args)


def count_kernel(temp_ref, bias_ref, i_ref, t_ref, sums_in, sums_ref):
    temp, bias = jnp.exp(temp_ref[...]), bias_ref[...]
    sums_ref[...] = sums_in[...]
    i_n = normal(i_ref[...])[0].astype(BF16)
    t_n = normal(t_ref[...])[0].astype(BF16)
    off_diagonal(i_n, t_n, temp, bias, sums_ref)


def count(temp, bias, i, t, sums):
    return pl.pallas_call(
        count_kernel,
        out_shape=jax.ShapeDtypeStruct((24, 128), F32),
        input_output_aliases={4: 0},
        compiler_params=pltpu.CompilerParams(vmem_limit_bytes=24 << 20),
        name="count",
    )(temp, bias, i, t, sums)


def last_kernel(temp_ref, bias_ref, img_n_ref, txt_n_ref, t_ref, i_ref, gimg_in, gtxt_in, img_ref, txt_ref, gimg_ref, gtxt_ref):
    temp, bias = jnp.exp(temp_ref[...]), bias_ref[...]
    for own_n, arrived, acc, own, out in (
        (img_n_ref, t_ref, gimg_in, img_ref, gimg_ref),
        (txt_n_ref, i_ref, gtxt_in, txt_ref, gtxt_ref),
    ):
        o_n = normal(arrived[...])[0].astype(BF16)
        g = off_diagonal(own_n[...], o_n, temp, bias)
        grad = acc[...] + jnp.dot(g, o_n, preferred_element_type=F32)
        unit, inv = normal(own[...])
        out[...] = inv * (grad - unit * jnp.sum(unit * grad, axis=-1, keepdims=True))


def last(temp, bias, own, t, i, acc, image, text):
    block = t.shape
    return pl.pallas_call(
        last_kernel,
        out_shape=(jax.ShapeDtypeStruct(block, F32),) * 2,
        compiler_params=pltpu.CompilerParams(vmem_limit_bytes=24 << 20),
        name="last",
    )(temp, bias, *own, t, i, *acc, image, text)


def exchange(values, axis, masks):
    length = lax.axis_size(axis)
    got = [lax.ppermute(values, axis, [(i, i ^ m) for i in range(length)]) for m in masks]
    return functools.reduce(jnp.add, got, values)


def body(image, text, log_temp, bias):
    temp, shift = log_temp.reshape(1, 1), bias.reshape(1, 1)
    pair_count = image.shape[0] * lax.axis_size("blk") * lax.axis_size("dp")
    t, i = {}, {}
    t[0], i[0] = text, image
    for s in (1, 2, 3, 4):
        t[s] = shifted(t[s - 1], 1)
        i[-s] = shifted(i[1 - s], -1)
        if s < 4:
            i[s] = shifted(i[s - 1], 1)
            t[-s] = shifted(t[1 - s], -1)

    img_n, txt_n, *acc, sums = own_tile(temp, shift, image, text)
    own = (img_n, txt_n)
    *acc, sums, i_m1 = pair(temp, shift, own, t[1], i[-1], acc, sums, keep=True)
    *acc, sums, i_1 = pair(temp, shift, own, t[-1], i[1], acc, sums, keep=True)
    *acc, sums = pair(temp, shift, own, t[2], i[-2], acc, sums, older=i_m1)
    sums = count(temp, shift, i[-2], t[2], sums)
    *acc, sums = pair(temp, shift, own, t[-2], i[2], acc, sums, older=i_1)
    for masks, axis in (((1, 8, 9), "dp"), ((2, 4, 6), "dp"), ((8, 16, 24), "blk"), ((1, 2, 3), "blk"), ((4,), "blk")):
        sums = exchange(sums, axis, masks)
    acc = pair(temp, shift, own, t[3], i[-3], acc)
    acc = pair(temp, shift, own, t[-3], i[3], acc)
    grad_image, grad_text = last(temp, shift, own, t[4], i[-4], acc, image, text)
    totals = jnp.sum(sums.reshape(3, -1), axis=1) / pair_count
    return (totals[0:1], totals[1:2], totals[2:3], grad_image, grad_text)


def solution(mesh):
    placed = (P(("blk", "dp"), None), P(("blk", "dp"), None), P(), P())
    return jax.shard_map(
        body,
        mesh=mesh,
        in_specs=placed,
        out_specs=(P(), P(), P(), P(("blk", "dp"), None), P(("blk", "dp"), None)),
        check_vma=False,
    )
```

time: 549 us -> 174 us (0.32)
  the two profiles are of different devices: /device:TPU:1 before, /device:TPU:24 now
where the time goes in v1:
time: 174 us; the launch traced here: 173 us
  starting transfers between devices  105 us (60%)
  waiting for transfers between devices  38.4 us (22%)
  Pallas kernels  23.7 us (14%)
  local copies, waits for them, and re-layouts  2.82 us (2%)
  between operations  2.39 us (1%)
    ppermute x14, starting transfers between devices, shifted(): lax.ppermute(array, 'blk', [(i, (i + by) % length) for i in range(length)])  57.2 us
    ppermute x13, starting transfers between devices, exchange(): lax.ppermute(values, axis, [(i, i ^ m) for i in range(length)])  48.1 us
    ppermute x13, waiting for transfers between devices, exchange(): lax.ppermute(values, axis, [(i, i ^ m) for i in range(length)])  22.2 us
    pallas_call x6, Pallas kernels, pair(): pl.pallas_call(functools.partial(pair_kernel, older is not None, sums is...  16.5 us
    ppermute x14, waiting for transfers between devices, shifted(): lax.ppermute(array, 'blk', [(i, (i + by) % length) for i in range(length)])  16.2 us
    pallas_call x1, Pallas kernels, last(): pl.pallas_call(last_kernel, out_shape=(jax.ShapeDtypeStruct(block, F32),)...  4.84 us
  transfers between devices with their start and end apart: 27, of which 6 were waited for; matrix products, arithmetic and copies ran while one was open for 1% of the time, Pallas kernels for 9%

profile of v1, /device:TPU:24, one launch (start us, length us, event | category | flops | bytes accessed | tf_op | source)
XLA Modules:
  0.0 172.9 jit_solution(6438710896839944696)
XLA Ops:
  0.6 4.3 %collective-permute-start.4 = (bf16[256,1152]{1,0:T(8,128)(2,1)}, bf16[256,1152]{1,0:T(8,128)(2,1)S(1)}, u32[]{:S(2)}, u32[]{:S(2)}) collective-permute-start(bf16[256,1152]{1,0:T(8,128)(2,1)} %txt_ref.3), channel_id=1, source_target_pairs={{0,16},{16,32},{32,48},{48,64},{64,80},{80,96},{96,112},{112,128},... | collective-permute-start | bytes 1769480 | tf_op jit(solution)/shard_map/ppermute | solution.py:15
  4.9 8.5 %collective-permute-start.6 = (bf16[256,1152]{1,0:T(8,128)(2,1)}, bf16[256,1152]{1,0:T(8,128)(2,1)S(1)}, u32[]{:S(2)}, u32[]{:S(2)}) collective-permute-start(bf16[256,1152]{1,0:T(8,128)(2,1)} %img_ref.3), channel_id=1, source_target_pairs={{0,496},{16,0},{32,16},{48,32},{64,48},{80,64},{96,80},{112,96},{1... | collective-permute-start | bytes 1769480 | tf_op jit(solution)/shard_map/ppermute | solution.py:15
  13.4 3.9 %collective-permute-start = (bf16[256,1152]{1,0:T(8,128)(2,1)}, bf16[256,1152]{1,0:T(8,128)(2,1)S(1)}, u32[]{:S(2)}, u32[]{:S(2)}) collective-permute-start(bf16[256,1152]{1,0:T(8,128)(2,1)} %txt_ref.3), channel_id=1, source_target_pairs={{0,496},{16,0},{32,16},{48,32},{64,48},{80,64},{96,80},{112,96},{1... | collective-permute-start | bytes 1769480 | tf_op jit(solution)/shard_map/ppermute | solution.py:15
  17.3 1.9 %collective-permute-start.2 = (bf16[256,1152]{1,0:T(8,128)(2,1)}, bf16[256,1152]{1,0:T(8,128)(2,1)S(1)}, u32[]{:S(2)}, u32[]{:S(2)}) collective-permute-start(bf16[256,1152]{1,0:T(8,128)(2,1)} %img_ref.3), channel_id=1, source_target_pairs={{0,16},{16,32},{32,48},{48,64},{64,80},{80,96},{96,112},{112,128},... | collective-permute-start | bytes 1769480 | tf_op jit(solution)/shard_map/ppermute | solution.py:15
  19.3 6.6 %collective-permute-done.4.refs_4_ = bf16[256,1152]{1,0:T(8,128)(2,1)S(1)} collective-permute-done((bf16[256,1152]{1,0:T(8,128)(2,1)}, bf16[256,1152]{1,0:T(8,128)(2,1)S(1)}, u32[]{:S(2)}, u32[]{:S(2)}) %collective-permute-start.4) | collective-permute-done | bytes 589856 | tf_op jit(solution)/shard_map/ppermute | solution.py:15
  27.8 6.1 %collective-permute-start.7 = (bf16[256,1152]{1,0:T(8,128)(2,1)S(1)}, bf16[256,1152]{1,0:T(8,128)(2,1)S(1)}, u32[]{:S(2)}, u32[]{:S(2)}) collective-permute-start(bf16[256,1152]{1,0:T(8,128)(2,1)S(1)} %collective-permute-done.6.refs_5_), channel_id=1, source_target_pairs={{0,496},{16,0},{32,16},{48,32},{64,48},{80,64},{96,80},{112,96},{1... | collective-permute-start | bytes 1769480 | tf_op jit(solution)/shard_map/ppermute | solution.py:15
  33.8 6.2 %collective-permute-done.refs_4_ = bf16[256,1152]{1,0:T(8,128)(2,1)S(1)} collective-permute-done((bf16[256,1152]{1,0:T(8,128)(2,1)}, bf16[256,1152]{1,0:T(8,128)(2,1)S(1)}, u32[]{:S(2)}, u32[]{:S(2)}) %collective-permute-start) | collective-permute-done | bytes 589856 | tf_op jit(solution)/shard_map/ppermute | solution.py:15
  40.1 6.4 %collective-permute-start.1 = (bf16[256,1152]{1,0:T(8,128)(2,1)S(1)}, bf16[256,1152]{1,0:T(8,128)(2,1)}, u32[]{:S(2)}, u32[]{:S(2)}) collective-permute-start(bf16[256,1152]{1,0:T(8,128)(2,1)S(1)} %collective-permute-done.refs_4_), channel_id=1, source_target_pairs={{0,496},{16,0},{32,16},{48,32},{64,48},{80,64},{96,80},{112,96},{1... | collective-permute-start | bytes 1769480 | tf_op jit(solution)/shard_map/ppermute | solution.py:15
  53.4 2.1 %pair.6 = (f32[256,1152]{1,0:T(8,128)S(1)}, f32[256,1152]{1,0:T(8,128)S(1)}, f32[24,128]{1,0:T(8,128)S(1)}, bf16[256,1152]{1,0:T(8,128)(2,1)S(1)}) custom-call(f32[1,1]{1,0:T(1,128)} %bitcast.3.refs_0_, f32[1,1]{1,0:T(1,128)} %bitcast.12.refs_1_, ...), custom_call_target="tpu_custom_call", output_to_operand_aliasing={{0}: (6, {}), {1}: (7, {}), {2}: (8, {})} | custom-call | tf_op jit(solution)/shard_map/pair/pallas_call | solution.py:131
  55.5 2.1 %pair.7 = (f32[256,1152]{1,0:T(8,128)S(1)}, f32[256,1152]{1,0:T(8,128)S(1)}, f32[24,128]{1,0:T(8,128)S(1)}, bf16[256,1152]{1,0:T(8,128)(2,1)S(1)}) custom-call(f32[1,1]{1,0:T(1,128)} %bitcast.4.refs_0_, f32[1,1]{1,0:T(1,128)} %bitcast.13.refs_1_, ...), custom_call_target="tpu_custom_call", output_to_operand_aliasing={{0}: (6, {}), {1}: (7, {}), {2}: (8, {})} | custom-call | tf_op jit(solution)/shard_map/pair/pallas_call | solution.py:131
  57.6 2.3 %pair.8 = (f32[256,1152]{1,0:T(8,128)S(1)}, f32[256,1152]{1,0:T(8,128)S(1)}, f32[24,128]{1,0:T(8,128)S(1)}) custom-call(f32[1,1]{1,0:T(1,128)} %bitcast.5.refs_0_, f32[1,1]{1,0:T(1,128)} %bitcast.14.refs_1_, bf16[256,1152]{1,0:T(8,128)(2,1)S(1)} %get-tuple-element.30.refs_2_.img_n_ref, ...), custom_call_target="tpu_custom_call", output_to_operand_aliasing={{0}: (6, {}), {1}: (7, {}), {2}: (9, {})} | custom-call | tf_op jit(solution)/shard_map/pair/pallas_call | solution.py:131
  60.8 3.3 %collective-permute-done.1.refs_4_ = bf16[256,1152]{1,0:T(8,128)(2,1)} collective-permute-done((bf16[256,1152]{1,0:T(8,128)(2,1)S(1)}, bf16[256,1152]{1,0:T(8,128)(2,1)}, u32[]{:S(2)}, u32[]{:S(2)}) %collective-permute-start.1) | collective-permute-done | bytes 589856 | tf_op jit(solution)/shard_map/ppermute | solution.py:15
  64.1 3.5 %pair.9 = (f32[256,1152]{1,0:T(8,128)S(1)}, f32[256,1152]{1,0:T(8,128)S(1)}, f32[24,128]{1,0:T(8,128)S(1)}) custom-call(f32[1,1]{1,0:T(1,128)} %bitcast.7.refs_0_, f32[1,1]{1,0:T(1,128)} %bitcast.16.refs_1_, bf16[256,1152]{1,0:T(8,128)(2,1)S(1)} %get-tuple-element.30.refs_2_.img_n_ref, ...), custom_call_target="tpu_custom_call", output_to_operand_aliasing={{0}: (6, {}), {1}: (7, {}), {2}: (9, {})} | custom-call | tf_op jit(solution)/shard_map/pair/pallas_call | solution.py:131
  67.6 4.5 %collective-permute-start.10 = (f32[24,128]{1,0:T(8,128)S(1)}, f32[24,128]{1,0:T(8,128)S(1)}, u32[]{:S(2)}, u32[]{:S(2)}) collective-permute-start(f32[24,128]{1,0:T(8,128)S(1)} %get-tuple-element.46), channel_id=1, source_target_pairs={{0,9},{1,8},{2,11},{3,10},{4,13},{5,12},{6,15},{7,14},{8,1},{9,0},... | collective-permute-start | bytes 36872 | tf_op jit(solution)/shard_map/ppermute | solution.py:183
  72.2 3.4 %collective-permute-start.8 = (f32[24,128]{1,0:T(8,128)S(1)}, f32[24,128]{1,0:T(8,128)S(1)}, u32[]{:S(2)}, u32[]{:S(2)}) collective-permute-start(f32[24,128]{1,0:T(8,128)S(1)} %get-tuple-element.46), channel_id=1, source_target_pairs={{0,1},{1,0},{2,3},{3,2},{4,5},{5,4},{6,7},{7,6},{8,9},{9,8},{10,11... | collective-permute-start | bytes 36872 | tf_op jit(solution)/shard_map/ppermute | solution.py:183
  75.6 3.8 %collective-permute-start.9 = (f32[24,128]{1,0:T(8,128)S(1)}, f32[24,128]{1,0:T(8,128)S(1)}, u32[]{:S(2)}, u32[]{:S(2)}) collective-permute-start(f32[24,128]{1,0:T(8,128)S(1)} %get-tuple-element.46), channel_id=1, source_target_pairs={{0,8},{1,9},{2,10},{3,11},{4,12},{5,13},{6,14},{7,15},{8,0},{9,1},... | collective-permute-start | bytes 36872 | tf_op jit(solution)/shard_map/ppermute | solution.py:183
  81.4 6.6 %collective-permute-start.23 = (bf16[256,1152]{1,0:T(8,128)(2,1)S(1)}, bf16[256,1152]{1,0:T(8,128)(2,1)}, u32[]{:S(2)}, u32[]{:S(2)}) collective-permute-start(bf16[256,1152]{1,0:T(8,128)(2,1)S(1)} %collective-permute-done.7.refs_5_.i_ref), channel_id=1, source_target_pairs={{0,496},{16,0},{32,16},{48,32},{64,48},{80,64},{96,80},{112,96},{1... | collective-permute-start | bytes 1769480 | tf_op jit(solution)/shard_map/ppermute | solution.py:15
  88.0 3.4 %collective-permute-start.11 = (f32[24,128]{1,0:T(8,128)S(1)}, f32[24,128]{1,0:T(8,128)S(1)}, u32[]{:S(2)}, u32[]{:S(2)}) collective-permute-start(f32[24,128]{1,0:T(8,128)S(1)} %add_add_fusion.3), channel_id=1, source_target_pairs={{0,2},{1,3},{2,0},{3,1},{4,6},{5,7},{6,4},{7,5},{8,10},{9,11},{10,... | collective-permute-start | bytes 36872 | tf_op jit(solution)/shard_map/ppermute | solution.py:183
  91.4 4.6 %collective-permute-start.12 = (f32[24,128]{1,0:T(8,128)S(1)}, f32[24,128]{1,0:T(8,128)S(1)}, u32[]{:S(2)}, u32[]{:S(2)}) collective-permute-start(f32[24,128]{1,0:T(8,128)S(1)} %add_add_fusion.3), channel_id=1, source_target_pairs={{0,4},{1,5},{2,6},{3,7},{4,0},{5,1},{6,2},{7,3},{8,12},{9,13},{10,... | collective-permute-start | bytes 36872 | tf_op jit(solution)/shard_map/ppermute | solution.py:183
  96.1 2.4 %collective-permute-start.13 = (f32[24,128]{1,0:T(8,128)S(1)}, f32[24,128]{1,0:T(8,128)S(1)}, u32[]{:S(2)}, u32[]{:S(2)}) collective-permute-start(f32[24,128]{1,0:T(8,128)S(1)} %add_add_fusion.3), channel_id=1, source_target_pairs={{0,6},{1,7},{2,4},{3,5},{4,2},{5,3},{6,0},{7,1},{8,14},{9,15},{10,... | collective-permute-start | bytes 36872 | tf_op jit(solution)/shard_map/ppermute | solution.py:183
  98.5 4.3 %collective-permute-done.13 = f32[24,128]{1,0:T(8,128)S(1)} collective-permute-done((f32[24,128]{1,0:T(8,128)S(1)}, f32[24,128]{1,0:T(8,128)S(1)}, u32[]{:S(2)}, u32[]{:S(2)}) %collective-permute-start.13) | collective-permute-done | bytes 12320 | tf_op jit(solution)/shard_map/ppermute | solution.py:183
  102.9 2.3 %collective-permute-start.14 = (f32[24,128]{1,0:T(8,128)S(1)}, f32[24,128]{1,0:T(8,128)S(1)}, u32[]{:S(2)}, u32[]{:S(2)}) collective-permute-start(f32[24,128]{1,0:T(8,128)S(1)} %add_add_fusion.2), channel_id=1, source_target_pairs={{0,128},{16,144},{32,160},{48,176},{64,192},{80,208},{96,224},{112... | collective-permute-start | bytes 36872 | tf_op jit(solution)/shard_map/ppermute | solution.py:183
  105.2 9.5 %collective-permute-start.15 = (f32[24,128]{1,0:T(8,128)S(1)}, f32[24,128]{1,0:T(8,128)S(1)}, u32[]{:S(2)}, u32[]{:S(2)}) collective-permute-start(f32[24,128]{1,0:T(8,128)S(1)} %add_add_fusion.2), channel_id=1, source_target_pairs={{0,256},{16,272},{32,288},{48,304},{64,320},{80,336},{96,352},{112... | collective-permute-start | bytes 36872 | tf_op jit(solution)/shard_map/ppermute | solution.py:183
  116.7 5.4 %collective-permute-done.16 = f32[24,128]{1,0:T(8,128)S(1)} collective-permute-done((f32[24,128]{1,0:T(8,128)S(1)}, f32[24,128]{1,0:T(8,128)S(1)}, u32[]{:S(2)}, u32[]{:S(2)}) %collective-permute-start.16) | collective-permute-done | bytes 12320 | tf_op jit(solution)/shard_map/ppermute | solution.py:183
  126.0 6.3 %collective-permute-start.19 = (f32[24,128]{1,0:T(8,128)S(1)}, f32[24,128]{1,0:T(8,128)S(1)}, u32[]{:S(2)}, u32[]{:S(2)}) collective-permute-start(f32[24,128]{1,0:T(8,128)S(1)} %add_add_fusion.1), channel_id=1, source_target_pairs={{0,48},{16,32},{32,16},{48,0},{64,112},{80,96},{96,80},{112,64},{1... | collective-permute-start | bytes 36872 | tf_op jit(solution)/shard_map/ppermute | solution.py:183
  134.2 3.9 %collective-permute-start.26 = (bf16[256,1152]{1,0:T(8,128)(2,1)}, bf16[256,1152]{1,0:T(8,128)(2,1)}, u32[]{:S(2)}, u32[]{:S(2)}) collective-permute-start(bf16[256,1152]{1,0:T(8,128)(2,1)} %collective-permute-done.3.refs_5_), channel_id=1, source_target_pairs={{0,16},{16,32},{32,48},{48,64},{64,80},{80,96},{96,112},{112,128},... | collective-permute-start | bytes 1769480 | tf_op jit(solution)/shard_map/ppermute | solution.py:15
  140.1 6.0 %collective-permute-start.24 = (bf16[256,1152]{1,0:T(8,128)(2,1)}, bf16[256,1152]{1,0:T(8,128)(2,1)}, u32[]{:S(2)}, u32[]{:S(2)}) collective-permute-start(bf16[256,1152]{1,0:T(8,128)(2,1)} %collective-permute-done.23.refs_5_), channel_id=1, source_target_pairs={{0,496},{16,0},{32,16},{48,32},{64,48},{80,64},{96,80},{112,96},{1... | collective-permute-start | bytes 1769480 | tf_op jit(solution)/shard_map/ppermute | solution.py:15
  146.1 2.1 %collective-permute-start.20 = (f32[24,128]{1,0:T(8,128)S(1)}, f32[24,128]{1,0:T(8,128)S(1)}, u32[]{:S(2)}, u32[]{:S(2)}) collective-permute-start(f32[24,128]{1,0:T(8,128)S(1)} %add_add_fusion), channel_id=1, source_target_pairs={{0,64},{16,80},{32,96},{48,112},{64,0},{80,16},{96,32},{112,48},{1... | collective-permute-start | bytes 36872 | tf_op jit(solution)/shard_map/ppermute | solution.py:183
  148.3 12.4 %collective-permute-done.20 = f32[24,128]{1,0:T(8,128)S(1)} collective-permute-done((f32[24,128]{1,0:T(8,128)S(1)}, f32[24,128]{1,0:T(8,128)S(1)}, u32[]{:S(2)}, u32[]{:S(2)}) %collective-permute-start.20) | collective-permute-done | bytes 12320 | tf_op jit(solution)/shard_map/ppermute | solution.py:183
  161.5 3.2 %pair.10 = (f32[256,1152]{1,0:T(8,128)S(1)}, f32[256,1152]{1,0:T(8,128)S(1)}) custom-call(f32[1,1]{1,0:T(1,128)} %bitcast.8.refs_0_, f32[1,1]{1,0:T(1,128)} %bitcast.17.refs_1_, bf16[256,1152]{1,0:T(8,128)(2,1)S(1)} %get-tuple-element.30.refs_2_.img_n_ref, ...), custom_call_target="tpu_custom_call", output_to_operand_aliasing={{0}: (6, {}), {1}: (7, {})} | custom-call | tf_op jit(solution)/shard_map/pair/pallas_call | solution.py:131
  164.8 3.3 %pair.11 = (f32[256,1152]{1,0:T(8,128)S(1)}, f32[256,1152]{1,0:T(8,128)S(1)}) custom-call(f32[1,1]{1,0:T(1,128)} %bitcast.9.refs_0_, f32[1,1]{1,0:T(1,128)} %bitcast.18.refs_1_, bf16[256,1152]{1,0:T(8,128)(2,1)S(1)} %get-tuple-element.30.refs_2_.img_n_ref, ...), custom_call_target="tpu_custom_call", output_to_operand_aliasing={{0}: (6, {}), {1}: (7, {})} | custom-call | tf_op jit(solution)/shard_map/pair/pallas_call | solution.py:131
  168.1 4.8 %last.1 = (f32[256,1152]{1,0:T(8,128)}, f32[256,1152]{1,0:T(8,128)}) custom-call(f32[1,1]{1,0:T(1,128)} %bitcast.10.temp_ref, f32[1,1]{1,0:T(1,128)} %bitcast.19.bias_ref, bf16[256,1152]{1,0:T(8,128)(2,1)S(1)} %get-tuple-element.30.refs_2_.img_n_ref, bf16[256,1152]{1,0:T(8,128)(2,1)S(1)} %get-tuple-element.31.refs_3_.txt_n_ref, ...), custom_call_target="tpu_custom_call" | custom-call | tf_op jit(solution)/shard_map/last/pallas_call | solution.py:173
  (48 shorter events, 20.9 us)
Async XLA Ops:
  0.6 25.2 %collective-permute-start.4 = (bf16[256,1152]{1,0:T(8,128)(2,1)}, bf16[256,1152]{1,0:T(8,128)(2,1)S(1)}, u32[]{:S(2)}, u32[]{:S(2)}) collective-permute-start(bf16[256,1152]{1,0:T(8,128)(2,1)} %txt_ref.3), channel_id=1, source_target_pairs={{0,16},{16,32},{32,48},{48,64},{64,80},{80,96},{96,112},{112,128},... | collective-permute-start | bytes 1769480 | tf_op jit(solution)/shard_map/ppermute | solution.py:15
  4.9 22.8 %collective-permute-start.6 = (bf16[256,1152]{1,0:T(8,128)(2,1)}, bf16[256,1152]{1,0:T(8,128)(2,1)S(1)}, u32[]{:S(2)}, u32[]{:S(2)}) collective-permute-start(bf16[256,1152]{1,0:T(8,128)(2,1)} %img_ref.3), channel_id=1, source_target_pairs={{0,496},{16,0},{32,16},{48,32},{64,48},{80,64},{96,80},{112,96},{1... | collective-permute-start | bytes 1769480 | tf_op jit(solution)/shard_map/ppermute | solution.py:15
  13.4 26.7 %collective-permute-start = (bf16[256,1152]{1,0:T(8,128)(2,1)}, bf16[256,1152]{1,0:T(8,128)(2,1)S(1)}, u32[]{:S(2)}, u32[]{:S(2)}) collective-permute-start(bf16[256,1152]{1,0:T(8,128)(2,1)} %txt_ref.3), channel_id=1, source_target_pairs={{0,496},{16,0},{32,16},{48,32},{64,48},{80,64},{96,80},{112,96},{1... | collective-permute-start | bytes 1769480 | tf_op jit(solution)/shard_map/ppermute | solution.py:15
  17.3 29.1 %collective-permute-start.2 = (bf16[256,1152]{1,0:T(8,128)(2,1)}, bf16[256,1152]{1,0:T(8,128)(2,1)S(1)}, u32[]{:S(2)}, u32[]{:S(2)}) collective-permute-start(bf16[256,1152]{1,0:T(8,128)(2,1)} %img_ref.3), channel_id=1, source_target_pairs={{0,16},{16,32},{32,48},{48,64},{64,80},{80,96},{96,112},{112,128},... | collective-permute-start | bytes 1769480 | tf_op jit(solution)/shard_map/ppermute | solution.py:15
  25.8 31.8 %collective-permute-start.5 = (bf16[256,1152]{1,0:T(8,128)(2,1)S(1)}, bf16[256,1152]{1,0:T(8,128)(2,1)S(1)}, u32[]{:S(2)}, u32[]{:S(2)}) collective-permute-start(bf16[256,1152]{1,0:T(8,128)(2,1)S(1)} %collective-permute-done.4.refs_4_), channel_id=1, source_target_pairs={{0,16},{16,32},{32,48},{48,64},{64,80},{80,96},{96,112},{112,128},... | collective-permute-start | bytes 1769480 | tf_op jit(solution)/shard_map/ppermute | solution.py:15
  27.8 29.9 %collective-permute-start.7 = (bf16[256,1152]{1,0:T(8,128)(2,1)S(1)}, bf16[256,1152]{1,0:T(8,128)(2,1)S(1)}, u32[]{:S(2)}, u32[]{:S(2)}) collective-permute-start(bf16[256,1152]{1,0:T(8,128)(2,1)S(1)} %collective-permute-done.6.refs_5_), channel_id=1, source_target_pairs={{0,496},{16,0},{32,16},{48,32},{64,48},{80,64},{96,80},{112,96},{1... | collective-permute-start | bytes 1769480 | tf_op jit(solution)/shard_map/ppermute | solution.py:15
  40.1 24.0 %collective-permute-start.1 = (bf16[256,1152]{1,0:T(8,128)(2,1)S(1)}, bf16[256,1152]{1,0:T(8,128)(2,1)}, u32[]{:S(2)}, u32[]{:S(2)}) collective-permute-start(bf16[256,1152]{1,0:T(8,128)(2,1)S(1)} %collective-permute-done.refs_4_), channel_id=1, source_target_pairs={{0,496},{16,0},{32,16},{48,32},{64,48},{80,64},{96,80},{112,96},{1... | collective-permute-start | bytes 1769480 | tf_op jit(solution)/shard_map/ppermute | solution.py:15
  46.5 17.6 %collective-permute-start.3 = (bf16[256,1152]{1,0:T(8,128)(2,1)S(1)}, bf16[256,1152]{1,0:T(8,128)(2,1)}, u32[]{:S(2)}, u32[]{:S(2)}) collective-permute-start(bf16[256,1152]{1,0:T(8,128)(2,1)S(1)} %collective-permute-done.2.refs_5_), channel_id=1, source_target_pairs={{0,16},{16,32},{32,48},{48,64},{64,80},{80,96},{96,112},{112,128},... | collective-permute-start | bytes 1769480 | tf_op jit(solution)/shard_map/ppermute | solution.py:15
  49.7 1.1 copy-start
  50.8 1.1 copy-start.2
  67.6 20.3 %collective-permute-start.10 = (f32[24,128]{1,0:T(8,128)S(1)}, f32[24,128]{1,0:T(8,128)S(1)}, u32[]{:S(2)}, u32[]{:S(2)}) collective-permute-start(f32[24,128]{1,0:T(8,128)S(1)} %get-tuple-element.46), channel_id=1, source_target_pairs={{0,9},{1,8},{2,11},{3,10},{4,13},{5,12},{6,15},{7,14},{8,1},{9,0},... | collective-permute-start | bytes 36872 | tf_op jit(solution)/shard_map/ppermute | solution.py:183
  72.2 15.8 %collective-permute-start.8 = (f32[24,128]{1,0:T(8,128)S(1)}, f32[24,128]{1,0:T(8,128)S(1)}, u32[]{:S(2)}, u32[]{:S(2)}) collective-permute-start(f32[24,128]{1,0:T(8,128)S(1)} %get-tuple-element.46), channel_id=1, source_target_pairs={{0,1},{1,0},{2,3},{3,2},{4,5},{5,4},{6,7},{7,6},{8,9},{9,8},{10,11... | collective-permute-start | bytes 36872 | tf_op jit(solution)/shard_map/ppermute | solution.py:183
  75.6 12.4 %collective-permute-start.9 = (f32[24,128]{1,0:T(8,128)S(1)}, f32[24,128]{1,0:T(8,128)S(1)}, u32[]{:S(2)}, u32[]{:S(2)}) collective-permute-start(f32[24,128]{1,0:T(8,128)S(1)} %get-tuple-element.46), channel_id=1, source_target_pairs={{0,8},{1,9},{2,10},{3,11},{4,12},{5,13},{6,14},{7,15},{8,0},{9,1},... | collective-permute-start | bytes 36872 | tf_op jit(solution)/shard_map/ppermute | solution.py:183
  79.4 58.7 %collective-permute-start.21 = (bf16[256,1152]{1,0:T(8,128)(2,1)S(1)}, bf16[256,1152]{1,0:T(8,128)(2,1)}, u32[]{:S(2)}, u32[]{:S(2)}) collective-permute-start(bf16[256,1152]{1,0:T(8,128)(2,1)S(1)} %collective-permute-done.5.refs_4_.t_ref), channel_id=1, source_target_pairs={{0,16},{16,32},{32,48},{48,64},{64,80},{80,96},{96,112},{112,128},... | collective-permute-start | bytes 1769480 | tf_op jit(solution)/shard_map/ppermute | solution.py:15
  81.4 58.7 %collective-permute-start.23 = (bf16[256,1152]{1,0:T(8,128)(2,1)S(1)}, bf16[256,1152]{1,0:T(8,128)(2,1)}, u32[]{:S(2)}, u32[]{:S(2)}) collective-permute-start(bf16[256,1152]{1,0:T(8,128)(2,1)S(1)} %collective-permute-done.7.refs_5_.i_ref), channel_id=1, source_target_pairs={{0,496},{16,0},{32,16},{48,32},{64,48},{80,64},{96,80},{112,96},{1... | collective-permute-start | bytes 1769480 | tf_op jit(solution)/shard_map/ppermute | solution.py:15
  88.0 10.4 %collective-permute-start.11 = (f32[24,128]{1,0:T(8,128)S(1)}, f32[24,128]{1,0:T(8,128)S(1)}, u32[]{:S(2)}, u32[]{:S(2)}) collective-permute-start(f32[24,128]{1,0:T(8,128)S(1)} %add_add_fusion.3), channel_id=1, source_target_pairs={{0,2},{1,3},{2,0},{3,1},{4,6},{5,7},{6,4},{7,5},{8,10},{9,11},{10,... | collective-permute-start | bytes 36872 | tf_op jit(solution)/shard_map/ppermute | solution.py:183
  91.4 7.1 %collective-permute-start.12 = (f32[24,128]{1,0:T(8,128)S(1)}, f32[24,128]{1,0:T(8,128)S(1)}, u32[]{:S(2)}, u32[]{:S(2)}) collective-permute-start(f32[24,128]{1,0:T(8,128)S(1)} %add_add_fusion.3), channel_id=1, source_target_pairs={{0,4},{1,5},{2,6},{3,7},{4,0},{5,1},{6,2},{7,3},{8,12},{9,13},{10,... | collective-permute-start | bytes 36872 | tf_op jit(solution)/shard_map/ppermute | solution.py:183
  96.1 6.8 %collective-permute-start.13 = (f32[24,128]{1,0:T(8,128)S(1)}, f32[24,128]{1,0:T(8,128)S(1)}, u32[]{:S(2)}, u32[]{:S(2)}) collective-permute-start(f32[24,128]{1,0:T(8,128)S(1)} %add_add_fusion.3), channel_id=1, source_target_pairs={{0,6},{1,7},{2,4},{3,5},{4,2},{5,3},{6,0},{7,1},{8,14},{9,15},{10,... | collective-permute-start | bytes 36872 | tf_op jit(solution)/shard_map/ppermute | solution.py:183
  102.9 13.8 %collective-permute-start.14 = (f32[24,128]{1,0:T(8,128)S(1)}, f32[24,128]{1,0:T(8,128)S(1)}, u32[]{:S(2)}, u32[]{:S(2)}) collective-permute-start(f32[24,128]{1,0:T(8,128)S(1)} %add_add_fusion.2), channel_id=1, source_target_pairs={{0,128},{16,144},{32,160},{48,176},{64,192},{80,208},{96,224},{112... | collective-permute-start | bytes 36872 | tf_op jit(solution)/shard_map/ppermute | solution.py:183
  105.2 11.4 %collective-permute-start.15 = (f32[24,128]{1,0:T(8,128)S(1)}, f32[24,128]{1,0:T(8,128)S(1)}, u32[]{:S(2)}, u32[]{:S(2)}) collective-permute-start(f32[24,128]{1,0:T(8,128)S(1)} %add_add_fusion.2), channel_id=1, source_target_pairs={{0,256},{16,272},{32,288},{48,304},{64,320},{80,336},{96,352},{112... | collective-permute-start | bytes 36872 | tf_op jit(solution)/shard_map/ppermute | solution.py:183
  114.7 7.4 %collective-permute-start.16 = (f32[24,128]{1,0:T(8,128)S(1)}, f32[24,128]{1,0:T(8,128)S(1)}, u32[]{:S(2)}, u32[]{:S(2)}) collective-permute-start(f32[24,128]{1,0:T(8,128)S(1)} %add_add_fusion.2), channel_id=1, source_target_pairs={{0,384},{16,400},{32,416},{48,432},{64,448},{80,464},{96,480},{112... | collective-permute-start | bytes 36872 | tf_op jit(solution)/shard_map/ppermute | solution.py:183
  122.1 10.1 %collective-permute-start.17 = (f32[24,128]{1,0:T(8,128)S(1)}, f32[24,128]{1,0:T(8,128)S(1)}, u32[]{:S(2)}, u32[]{:S(2)}) collective-permute-start(f32[24,128]{1,0:T(8,128)S(1)} %add_add_fusion.1), channel_id=1, source_target_pairs={{0,16},{16,0},{32,48},{48,32},{64,80},{80,64},{96,112},{112,96},{1... | collective-permute-start | bytes 36872 | tf_op jit(solution)/shard_map/ppermute | solution.py:183
  124.0 10.2 %collective-permute-start.18 = (f32[24,128]{1,0:T(8,128)S(1)}, f32[24,128]{1,0:T(8,128)S(1)}, u32[]{:S(2)}, u32[]{:S(2)}) collective-permute-start(f32[24,128]{1,0:T(8,128)S(1)} %add_add_fusion.1), channel_id=1, source_target_pairs={{0,32},{16,48},{32,0},{48,16},{64,96},{80,112},{96,64},{112,80},{1... | collective-permute-start | bytes 36872 | tf_op jit(solution)/shard_map/ppermute | solution.py:183
  126.0 20.2 %collective-permute-start.19 = (f32[24,128]{1,0:T(8,128)S(1)}, f32[24,128]{1,0:T(8,128)S(1)}, u32[]{:S(2)}, u32[]{:S(2)}) collective-permute-start(f32[24,128]{1,0:T(8,128)S(1)} %add_add_fusion.1), channel_id=1, source_target_pairs={{0,48},{16,32},{32,16},{48,0},{64,112},{80,96},{96,80},{112,64},{1... | collective-permute-start | bytes 36872 | tf_op jit(solution)/shard_map/ppermute | solution.py:183
  132.3 32.5 %collective-permute-start.25 = (bf16[256,1152]{1,0:T(8,128)(2,1)}, bf16[256,1152]{1,0:T(8,128)(2,1)}, u32[]{:S(2)}, u32[]{:S(2)}) collective-permute-start(bf16[256,1152]{1,0:T(8,128)(2,1)} %collective-permute-done.1.refs_4_), channel_id=1, source_target_pairs={{0,496},{16,0},{32,16},{48,32},{64,48},{80,64},{96,80},{112,96},{1... | collective-permute-start | bytes 1769480 | tf_op jit(solution)/shard_map/ppermute | solution.py:15
  134.2 30.5 %collective-permute-start.26 = (bf16[256,1152]{1,0:T(8,128)(2,1)}, bf16[256,1152]{1,0:T(8,128)(2,1)}, u32[]{:S(2)}, u32[]{:S(2)}) collective-permute-start(bf16[256,1152]{1,0:T(8,128)(2,1)} %collective-permute-done.3.refs_5_), channel_id=1, source_target_pairs={{0,16},{16,32},{32,48},{48,64},{64,80},{80,96},{96,112},{112,128},... | collective-permute-start | bytes 1769480 | tf_op jit(solution)/shard_map/ppermute | solution.py:15
  138.1 29.9 %collective-permute-start.22 = (bf16[256,1152]{1,0:T(8,128)(2,1)}, bf16[256,1152]{1,0:T(8,128)(2,1)}, u32[]{:S(2)}, u32[]{:S(2)}) collective-permute-start(bf16[256,1152]{1,0:T(8,128)(2,1)} %collective-permute-done.21.refs_4_), channel_id=1, source_target_pairs={{0,16},{16,32},{32,48},{48,64},{64,80},{80,96},{96,112},{112,128},... | collective-permute-start | bytes 1769480 | tf_op jit(solution)/shard_map/ppermute | solution.py:15
  140.1 28.0 %collective-permute-start.24 = (bf16[256,1152]{1,0:T(8,128)(2,1)}, bf16[256,1152]{1,0:T(8,128)(2,1)}, u32[]{:S(2)}, u32[]{:S(2)}) collective-permute-start(bf16[256,1152]{1,0:T(8,128)(2,1)} %collective-permute-done.23.refs_5_), channel_id=1, source_target_pairs={{0,496},{16,0},{32,16},{48,32},{64,48},{80,64},{96,80},{112,96},{1... | collective-permute-start | bytes 1769480 | tf_op jit(solution)/shard_map/ppermute | solution.py:15
  146.1 14.5 %collective-permute-start.20 = (f32[24,128]{1,0:T(8,128)S(1)}, f32[24,128]{1,0:T(8,128)S(1)}, u32[]{:S(2)}, u32[]{:S(2)}) collective-permute-start(f32[24,128]{1,0:T(8,128)S(1)} %add_add_fusion), channel_id=1, source_target_pairs={{0,64},{16,80},{32,96},{48,112},{64,0},{80,16},{96,32},{112,48},{1... | collective-permute-start | bytes 36872 | tf_op jit(solution)/shard_map/ppermute | solution.py:183
  164.7 3.3 %copy-start.1 = (bf16[256,1152]{1,0:T(8,128)(2,1)S(1)}, bf16[256,1152]{1,0:T(8,128)(2,1)}, u32[]{:S(2)}) copy-start(bf16[256,1152]{1,0:T(8,128)(2,1)} %img_ref.3) | copy-start | bytes 1769476
  164.7 3.3 %copy-start.3 = (bf16[256,1152]{1,0:T(8,128)(2,1)S(1)}, bf16[256,1152]{1,0:T(8,128)(2,1)}, u32[]{:S(2)}) copy-start(bf16[256,1152]{1,0:T(8,128)(2,1)} %txt_ref.3) | copy-start | bytes 1769476

commit v2 on v1

--- a/solution.py
+++ b/solution.py
@@ -8,6 +8,7 @@
 from jax.sharding import PartitionSpec as P
 
 F32, BF16 = jnp.float32, jnp.bfloat16
+COST_LAST, COST_PAIR = 2 * 10**9, 10**9
 
 
 def shifted(array, by):
@@ -32,6 +33,10 @@
 def fold(v):
     r = jnp.sum(v.reshape(v.shape[0] // 8, 8, v.shape[1]), axis=0)
     return sum(r[:, i : i + 128] for i in range(0, v.shape[1], 128))
+
+
+def cost(flops):
+    return pl.CostEstimate(flops=flops, bytes_accessed=8 << 20, transcendentals=1 << 17)
 
 
 def add_terms(sums_ref, u, dl, scaled):
@@ -133,6 +138,7 @@
         out_shape=tuple(outs),
         input_output_aliases=aliases,
         compiler_params=pltpu.CompilerParams(vmem_limit_bytes=24 << 20),
+        cost_estimate=cost(COST_PAIR),
         name="pair",
     )(*args)
 
@@ -174,42 +180,74 @@
         last_kernel,
         out_shape=(jax.ShapeDtypeStruct(block, F32),) * 2,
         compiler_params=pltpu.CompilerParams(vmem_limit_bytes=24 << 20),
+        cost_estimate=cost(COST_LAST),
         name="last",
     )(temp, bias, *own, t, i, *acc, image, text)
 
 
-def exchange(values, axis, masks):
-    length = lax.axis_size(axis)
-    got = [lax.ppermute(values, axis, [(i, i ^ m) for i in range(length)]) for m in masks]
-    return functools.reduce(jnp.add, got, values)
+def spread_kernel(parts_ref, out_ref):
+    out_ref[...] = jnp.broadcast_to(jnp.sum(parts_ref[...], axis=0)[None], out_ref.shape)
+
+
+def spread(parts, copies):
+    return pl.pallas_call(
+        spread_kernel,
+        out_shape=jax.ShapeDtypeStruct((copies,) + parts.shape[1:], F32),
+        compiler_params=pltpu.CompilerParams(vmem_limit_bytes=8 << 20),
+        name="spread",
+    )(parts)
+
+
+def finish_kernel(pair_count, parts_ref, *out_refs):
+    total = jnp.sum(parts_ref[...], axis=0)
+    for k, out_ref in enumerate(out_refs):
+        out_ref[...] = jnp.sum(total[8 * k : 8 * k + 8], keepdims=True) / pair_count
+
+
+def finish(parts, pair_count):
+    totals = pl.pallas_call(
+        functools.partial(finish_kernel, pair_count),
+        out_shape=(jax.ShapeDtypeStruct((1, 1), F32),) * 3,
+        compiler_params=pltpu.CompilerParams(vmem_limit_bytes=8 << 20),
+        name="finish",
+    )(parts)
+    return tuple(total.reshape(1) for total in totals)
+
+
+def to_all(parts, axis):
+    return lax.all_to_all(parts, axis, 0, 0)
 
 
 def body(image, text, log_temp, bias):
     temp, shift = log_temp.reshape(1, 1), bias.reshape(1, 1)
     pair_count = image.shape[0] * lax.axis_size("blk") * lax.axis_size("dp")
-    t, i = {}, {}
-    t[0], i[0] = text, image
-    for s in (1, 2, 3, 4):
-        t[s] = shifted(t[s - 1], 1)
-        i[-s] = shifted(i[1 - s], -1)
-        if s < 4:
-            i[s] = shifted(i[s - 1], 1)
-            t[-s] = shifted(t[1 - s], -1)
-
+    after = lax.optimization_barrier
+    t, i = {0: text}, {0: image}
+    t[1], i[-1] = shifted(text, 1), shifted(image, -1)
+    i[1], t[-1] = shifted(image, 1), shifted(text, -1)
     img_n, txt_n, *acc, sums = own_tile(temp, shift, image, text)
+    t[1], i[-1], img_n, txt_n = after((t[1], i[-1], img_n, txt_n))
     own = (img_n, txt_n)
+    t[2], i[-2] = shifted(t[1], 1), shifted(i[-1], -1)
     *acc, sums, i_m1 = pair(temp, shift, own, t[1], i[-1], acc, sums, keep=True)
+    i[1], t[-1], sums = after((i[1], t[-1], sums))
+    i[2], t[-2] = shifted(i[1], 1), shifted(t[-1], -1)
     *acc, sums, i_1 = pair(temp, shift, own, t[-1], i[1], acc, sums, keep=True)
+    t[2], i[-2], sums = after((t[2], i[-2], sums))
+    t[3], i[-3] = shifted(t[2], 1), shifted(i[-2], -1)
     *acc, sums = pair(temp, shift, own, t[2], i[-2], acc, sums, older=i_m1)
     sums = count(temp, shift, i[-2], t[2], sums)
+    i[2], t[-2], sums = after((i[2], t[-2], sums))
+    i[3], t[-3] = shifted(i[2], 1), shifted(t[-2], -1)
     *acc, sums = pair(temp, shift, own, t[-2], i[2], acc, sums, older=i_1)
-    for masks, axis in (((1, 8, 9), "dp"), ((2, 4, 6), "dp"), ((8, 16, 24), "blk"), ((1, 2, 3), "blk"), ((4,), "blk")):
-        sums = exchange(sums, axis, masks)
+    parts = to_all(spread(sums[None], lax.axis_size("dp")), "dp")
+    t[4], i[-4] = shifted(t[3], 1), shifted(i[-3], -1)
+    i[3], t[-3], parts = after((i[3], t[-3], parts))
+    parts = to_all(spread(parts, lax.axis_size("blk")), "blk")
     acc = pair(temp, shift, own, t[3], i[-3], acc)
     acc = pair(temp, shift, own, t[-3], i[3], acc)
     grad_image, grad_text = last(temp, shift, own, t[4], i[-4], acc, image, text)
-    totals = jnp.sum(sums.reshape(3, -1), axis=1) / pair_count
-    return (totals[0:1], totals[1:2], totals[2:3], grad_image, grad_text)
+    return (*finish(parts, pair_count), grad_image, grad_text)
 
 
 def solution(mesh):

time: 174 us -> 133 us (0.76)
  the two profiles are of different devices: /device:TPU:24 before, /device:TPU:1 now
where the time goes in v2:
time: 133 us; the launch traced here: 131 us
  starting transfers between devices  79.3 us (60%)
  Pallas kernels  28.8 us (22%)
  waiting for transfers between devices  17 us (13%)
  local copies, waits for them, and re-layouts  3.54 us (3%)
  between operations  2.19 us (2%)
    ppermute x14, starting transfers between devices, shifted(): lax.ppermute(array, 'blk', [(i, (i + by) % length) for i in range(length)])  63.8 us
    pallas_call x6, Pallas kernels, pair(): pl.pallas_call(functools.partial(pair_kernel, older is not None, sums is...  17.8 us
    all_to_all x2, starting transfers between devices, to_all(): return lax.all_to_all(parts, axis, 0, 0)  15.5 us
    all_to_all x2, waiting for transfers between devices, to_all(): return lax.all_to_all(parts, axis, 0, 0)  8.64 us
    ppermute x14, waiting for transfers between devices, shifted(): lax.ppermute(array, 'blk', [(i, (i + by) % length) for i in range(length)])  8.31 us
    pallas_call x1, Pallas kernels, last(): pl.pallas_call(last_kernel, out_shape=(jax.ShapeDtypeStruct(block, F32),)...  4.84 us
    unnamed x12, local copies, waits for them, and re-layouts  3.54 us
  transfers between devices with their start and end apart: 16, of which 6 were waited for; matrix products, arithmetic and copies ran while one was open for 0% of the time, Pallas kernels for 21%

profile of v2, /device:TPU:1, one launch (start us, length us, event | category | flops | bytes accessed | tf_op | source)
XLA Modules:
  0.0 130.8 jit_solution(1589779465060934459)
XLA Ops:
  0.6 14.5 %collective-permute-start.3 = (bf16[256,1152]{1,0:T(8,128)(2,1)}, bf16[256,1152]{1,0:T(8,128)(2,1)S(1)}, u32[]{:S(2)}, u32[]{:S(2)}) collective-permute-start(bf16[256,1152]{1,0:T(8,128)(2,1)} %img_ref.3), channel_id=1, source_target_pairs={{0,496},{16,0},{32,16},{48,32},{64,48},{80,64},{96,80},{112,96},{1... | collective-permute-start | bytes 1769480 | tf_op jit(solution)/shard_map/ppermute | solution.py:16
  15.2 1.9 %collective-permute-start.2 = (bf16[256,1152]{1,0:T(8,128)(2,1)}, bf16[256,1152]{1,0:T(8,128)(2,1)S(1)}, u32[]{:S(2)}, u32[]{:S(2)}) collective-permute-start(bf16[256,1152]{1,0:T(8,128)(2,1)} %txt_ref.3), channel_id=1, source_target_pairs={{0,16},{16,32},{32,48},{48,64},{64,80},{80,96},{96,112},{112,128},... | collective-permute-start | bytes 1769480 | tf_op jit(solution)/shard_map/ppermute | solution.py:16
  17.1 1.9 %collective-permute-start = (bf16[256,1152]{1,0:T(8,128)(2,1)}, bf16[256,1152]{1,0:T(8,128)(2,1)S(1)}, u32[]{:S(2)}, u32[]{:S(2)}) collective-permute-start(bf16[256,1152]{1,0:T(8,128)(2,1)} %img_ref.3), channel_id=1, source_target_pairs={{0,16},{16,32},{32,48},{48,64},{64,80},{80,96},{96,112},{112,128},... | collective-permute-start | bytes 1769480 | tf_op jit(solution)/shard_map/ppermute | solution.py:16
  19.0 7.3 %collective-permute-start.1 = (bf16[256,1152]{1,0:T(8,128)(2,1)}, bf16[256,1152]{1,0:T(8,128)(2,1)S(1)}, u32[]{:S(2)}, u32[]{:S(2)}) collective-permute-start(bf16[256,1152]{1,0:T(8,128)(2,1)} %txt_ref.3), channel_id=1, source_target_pairs={{0,496},{16,0},{32,16},{48,32},{64,48},{80,64},{96,80},{112,96},{1... | collective-permute-start | bytes 1769480 | tf_op jit(solution)/shard_map/ppermute | solution.py:16
  29.7 1.6 %own_tile.1 = (bf16[256,1152]{1,0:T(8,128)(2,1)S(1)}, bf16[256,1152]{1,0:T(8,128)(2,1)S(1)}, f32[256,1152]{1,0:T(8,128)S(1)}, f32[256,1152]{1,0:T(8,128)S(1)}, f32[24,128]{1,0:T(8,128)S(1)}) custom-call(f32[1,1]{1,0:T(1,128)} %bitcast.6.temp_ref, f32[1,1]{1,0:T(1,128)} %bitcast.15.bias_ref, bf16[256,1152]{1,0:T(8,128)(2,1)S(1)} %copy-done.2, ...), custom_call_target="tpu_custom_call" | custom-call | tf_op jit(solution)/shard_map/own_tile/pallas_call | solution.py:80
  31.3 3.8 %collective-permute-done.2.refs_4_ = bf16[256,1152]{1,0:T(8,128)(2,1)S(1)} collective-permute-done((bf16[256,1152]{1,0:T(8,128)(2,1)}, bf16[256,1152]{1,0:T(8,128)(2,1)S(1)}, u32[]{:S(2)}, u32[]{:S(2)}) %collective-permute-start.2) | collective-permute-done | bytes 589856 | tf_op jit(solution)/shard_map/ppermute | solution.py:16
  35.1 1.9 %collective-permute-start.6 = (bf16[256,1152]{1,0:T(8,128)(2,1)S(1)}, bf16[256,1152]{1,0:T(8,128)(2,1)}, u32[]{:S(2)}, u32[]{:S(2)}) collective-permute-start(bf16[256,1152]{1,0:T(8,128)(2,1)S(1)} %collective-permute-done.2.refs_4_), channel_id=1, source_target_pairs={{0,16},{16,32},{32,48},{48,64},{64,80},{80,96},{96,112},{112,128},... | collective-permute-start | bytes 1769480 | tf_op jit(solution)/shard_map/ppermute | solution.py:16
  37.0 7.3 %collective-permute-start.7 = (bf16[256,1152]{1,0:T(8,128)(2,1)S(1)}, bf16[256,1152]{1,0:T(8,128)(2,1)}, u32[]{:S(2)}, u32[]{:S(2)}) collective-permute-start(bf16[256,1152]{1,0:T(8,128)(2,1)S(1)} %collective-permute-done.3.refs_5_), channel_id=1, source_target_pairs={{0,496},{16,0},{32,16},{48,32},{64,48},{80,64},{96,80},{112,96},{1... | collective-permute-start | bytes 1769480 | tf_op jit(solution)/shard_map/ppermute | solution.py:16
  44.3 2.1 %pair.6 = (f32[256,1152]{1,0:T(8,128)S(1)}, f32[256,1152]{1,0:T(8,128)S(1)}, f32[24,128]{1,0:T(8,128)S(1)}, bf16[256,1152]{1,0:T(8,128)(2,1)S(1)}) custom-call(f32[1,1]{1,0:T(1,128)} %bitcast.7.refs_0_, f32[1,1]{1,0:T(1,128)} %bitcast.16.refs_1_, ...), custom_call_target="tpu_custom_call", output_to_operand_aliasing={{0}: (6, {}), {1}: (7, {}), {2}: (8, {})} | custom-call | flops 1000000000 | bytes 8388608 | tf_op jit(solution)/shard_map/pair/pallas_call | solution.py:136
  46.4 1.3 %collective-permute-done.refs_5_ = bf16[256,1152]{1,0:T(8,128)(2,1)S(1)} collective-permute-done((bf16[256,1152]{1,0:T(8,128)(2,1)}, bf16[256,1152]{1,0:T(8,128)(2,1)S(1)}, u32[]{:S(2)}, u32[]{:S(2)}) %collective-permute-start) | collective-permute-done | bytes 589856 | tf_op jit(solution)/shard_map/ppermute | solution.py:16
  47.7 1.9 %collective-permute-start.4 = (bf16[256,1152]{1,0:T(8,128)(2,1)S(1)}, bf16[256,1152]{1,0:T(8,128)(2,1)}, u32[]{:S(2)}, u32[]{:S(2)}) collective-permute-start(bf16[256,1152]{1,0:T(8,128)(2,1)S(1)} %collective-permute-done.refs_5_), channel_id=1, source_target_pairs={{0,16},{16,32},{32,48},{48,64},{64,80},{80,96},{96,112},{112,128},... | collective-permute-start | bytes 1769480 | tf_op jit(solution)/shard_map/ppermute | solution.py:16
  49.6 7.3 %collective-permute-start.5 = (bf16[256,1152]{1,0:T(8,128)(2,1)S(1)}, bf16[256,1152]{1,0:T(8,128)(2,1)}, u32[]{:S(2)}, u32[]{:S(2)}) collective-permute-start(bf16[256,1152]{1,0:T(8,128)(2,1)S(1)} %collective-permute-done.1.refs_4_), channel_id=1, source_target_pairs={{0,496},{16,0},{32,16},{48,32},{64,48},{80,64},{96,80},{112,96},{1... | collective-permute-start | bytes 1769480 | tf_op jit(solution)/shard_map/ppermute | solution.py:16
  56.9 2.1 %pair.7 = (f32[256,1152]{1,0:T(8,128)S(1)}, f32[256,1152]{1,0:T(8,128)S(1)}, f32[24,128]{1,0:T(8,128)S(1)}, bf16[256,1152]{1,0:T(8,128)(2,1)S(1)}) custom-call(f32[1,1]{1,0:T(1,128)} %bitcast.8.refs_0_, f32[1,1]{1,0:T(1,128)} %bitcast.17.refs_1_, ...), custom_call_target="tpu_custom_call", output_to_operand_aliasing={{0}: (6, {}), {1}: (7, {}), {2}: (8, {})} | custom-call | flops 1000000000 | bytes 8388608 | tf_op jit(solution)/shard_map/pair/pallas_call | solution.py:136
  59.0 1.4 %collective-permute-done.6.refs_4_.t_ref = bf16[256,1152]{1,0:T(8,128)(2,1)} collective-permute-done((bf16[256,1152]{1,0:T(8,128)(2,1)S(1)}, bf16[256,1152]{1,0:T(8,128)(2,1)}, u32[]{:S(2)}, u32[]{:S(2)}) %collective-permute-start.6) | collective-permute-done | bytes 589856 | tf_op jit(solution)/shard_map/ppermute | solution.py:16
  60.5 1.9 %collective-permute-start.12 = (bf16[256,1152]{1,0:T(8,128)(2,1)}, bf16[256,1152]{1,0:T(8,128)(2,1)}, u32[]{:S(2)}, u32[]{:S(2)}) collective-permute-start(bf16[256,1152]{1,0:T(8,128)(2,1)} %collective-permute-done.7.refs_5_.i_ref), channel_id=1, source_target_pairs={{0,496},{16,0},{32,16},{48,32},{64,48},{80,64},{96,80},{112,96},{1... | collective-permute-start | bytes 1769480 | tf_op jit(solution)/shard_map/ppermute | solution.py:16
  62.4 3.4 %collective-permute-start.10 = (bf16[256,1152]{1,0:T(8,128)(2,1)}, bf16[256,1152]{1,0:T(8,128)(2,1)}, u32[]{:S(2)}, u32[]{:S(2)}) collective-permute-start(bf16[256,1152]{1,0:T(8,128)(2,1)} %collective-permute-done.6.refs_4_.t_ref), channel_id=1, source_target_pairs={{0,16},{16,32},{32,48},{48,64},{64,80},{80,96},{96,112},{112,128},... | collective-permute-start | bytes 1769480 | tf_op jit(solution)/shard_map/ppermute | solution.py:16
  65.7 3.5 %pair.8 = (f32[256,1152]{1,0:T(8,128)S(1)}, f32[256,1152]{1,0:T(8,128)S(1)}, f32[24,128]{1,0:T(8,128)S(1)}) custom-call(f32[1,1]{1,0:T(1,128)} %bitcast.9.refs_0_, f32[1,1]{1,0:T(1,128)} %bitcast.18.refs_1_, bf16[256,1152]{1,0:T(8,128)(2,1)S(1)} %get-tuple-element.51.refs_2_.img_n_ref, ...), custom_call_target="tpu_custom_call", output_to_operand_aliasing={{0}: (6, {}), {1}: (7, {}), {2}: (9, {})} | custom-call | flops 1000000000 | bytes 8388608 | tf_op jit(solution)/shard_map/pair/pallas_call | solution.py:136
  69.3 2.0 %count.1.refs_9_ = f32[24,128]{1,0:T(8,128)S(1)} custom-call(f32[1,1]{1,0:T(1,128)} %bitcast.10.temp_ref, f32[1,1]{1,0:T(1,128)} %bitcast.19.bias_ref, bf16[256,1152]{1,0:T(8,128)(2,1)} %collective-permute-done.7.refs_5_.i_ref, bf16[256,1152]{1,0:T(8,128)(2,1)} %collective-permute-done.6.refs_4_.t_ref, ...), custom_call_target="tpu_custom_call", output_to_operand_aliasing={{}: (4, {})} | custom-call | tf_op jit(solution)/shard_map/count/pallas_call | solution.py:155
  71.3 1.8 %collective-permute-done.4.refs_5_ = bf16[256,1152]{1,0:T(8,128)(2,1)} collective-permute-done((bf16[256,1152]{1,0:T(8,128)(2,1)S(1)}, bf16[256,1152]{1,0:T(8,128)(2,1)}, u32[]{:S(2)}, u32[]{:S(2)}) %collective-permute-start.4) | collective-permute-done | bytes 589856 | tf_op jit(solution)/shard_map/ppermute | solution.py:16
  73.1 1.9 %collective-permute-start.8 = (bf16[256,1152]{1,0:T(8,128)(2,1)}, bf16[256,1152]{1,0:T(8,128)(2,1)}, u32[]{:S(2)}, u32[]{:S(2)}) collective-permute-start(bf16[256,1152]{1,0:T(8,128)(2,1)} %collective-permute-done.4.refs_5_), channel_id=1, source_target_pairs={{0,16},{16,32},{32,48},{48,64},{64,80},{80,96},{96,112},{112,128},... | collective-permute-start | bytes 1769480 | tf_op jit(solution)/shard_map/ppermute | solution.py:16
  75.0 7.3 %collective-permute-start.9 = (bf16[256,1152]{1,0:T(8,128)(2,1)}, bf16[256,1152]{1,0:T(8,128)(2,1)}, u32[]{:S(2)}, u32[]{:S(2)}) collective-permute-start(bf16[256,1152]{1,0:T(8,128)(2,1)} %collective-permute-done.5.refs_4_), channel_id=1, source_target_pairs={{0,496},{16,0},{32,16},{48,32},{64,48},{80,64},{96,80},{112,96},{1... | collective-permute-start | bytes 1769480 | tf_op jit(solution)/shard_map/ppermute | solution.py:16
  82.3 3.5 %pair.9 = (f32[256,1152]{1,0:T(8,128)S(1)}, f32[256,1152]{1,0:T(8,128)S(1)}, f32[24,128]{1,0:T(8,128)S(1)}) custom-call(f32[1,1]{1,0:T(1,128)} %bitcast.11.refs_0_, f32[1,1]{1,0:T(1,128)} %bitcast.20.refs_1_, bf16[256,1152]{1,0:T(8,128)(2,1)S(1)} %get-tuple-element.51.refs_2_.img_n_ref, ...), custom_call_target="tpu_custom_call", output_to_operand_aliasing={{0}: (6, {}), {1}: (7, {}), {2}: (9, {})} | custom-call | flops 1000000000 | bytes 8388608 | tf_op jit(solution)/shard_map/pair/pallas_call | solution.py:136
  86.5 10.8 %all-to-all-start = ((f32[16,24,128]{2,1,0:T(8,128)}), f32[16,24,128]{2,1,0:T(8,128)}, u32[]{:S(2)}, u32[]{:S(2)}) async-start(f32[16,24,128]{2,1,0:T(8,128)} %copy-done.1), calls=%async_computation | async-start | bytes 393216 | tf_op jit(solution)/shard_map/all_to_all | solution.py:218
  97.3 2.3 %collective-permute-start.13 = (bf16[256,1152]{1,0:T(8,128)(2,1)}, bf16[256,1152]{1,0:T(8,128)(2,1)}, u32[]{:S(2)}, u32[]{:S(2)}) collective-permute-start(bf16[256,1152]{1,0:T(8,128)(2,1)} %collective-permute-done.12.refs_5_), channel_id=1, source_target_pairs={{0,496},{16,0},{32,16},{48,32},{64,48},{80,64},{96,80},{112,96},{1... | collective-permute-start | bytes 1769480 | tf_op jit(solution)/shard_map/ppermute | solution.py:16
  99.7 2.9 %collective-permute-start.11 = (bf16[256,1152]{1,0:T(8,128)(2,1)}, bf16[256,1152]{1,0:T(8,128)(2,1)}, u32[]{:S(2)}, u32[]{:S(2)}) collective-permute-start(bf16[256,1152]{1,0:T(8,128)(2,1)} %collective-permute-done.10.refs_4_), channel_id=1, source_target_pairs={{0,16},{16,32},{32,48},{48,64},{64,80},{80,96},{96,112},{112,128},... | collective-permute-start | bytes 1769480 | tf_op jit(solution)/shard_map/ppermute | solution.py:16
  102.6 5.4 %all-to-all-done.parts_ref = f32[16,24,128]{2,1,0:T(8,128)} async-done(((f32[16,24,128]{2,1,0:T(8,128)}), f32[16,24,128]{2,1,0:T(8,128)}, u32[]{:S(2)}, u32[]{:S(2)}) %all-to-all-start) | async-done | bytes 196640 | tf_op jit(solution)/shard_map/all_to_all | solution.py:218
  109.7 4.8 %all-to-all-start.1 = ((f32[32,24,128]{2,1,0:T(8,128)}), f32[32,24,128]{2,1,0:T(8,128)}, u32[]{:S(2)}, u32[]{:S(2)}) async-start(f32[32,24,128]{2,1,0:T(8,128)} %copy-done), calls=%async_computation.1 | async-start | bytes 786432 | tf_op jit(solution)/shard_map/all_to_all | solution.py:218
  114.5 3.2 %pair.10 = (f32[256,1152]{1,0:T(8,128)S(1)}, f32[256,1152]{1,0:T(8,128)S(1)}) custom-call(f32[1,1]{1,0:T(1,128)} %bitcast.12.refs_0_, f32[1,1]{1,0:T(1,128)} %bitcast.21.refs_1_, bf16[256,1152]{1,0:T(8,128)(2,1)S(1)} %get-tuple-element.51.refs_2_.img_n_ref, ...), custom_call_target="tpu_custom_call", output_to_operand_aliasing={{0}: (6, {}), {1}: (7, {})} | custom-call | flops 1000000000 | bytes 8388608 | tf_op jit(solution)/shard_map/pair/pallas_call | solution.py:136
  117.7 3.3 %pair.11 = (f32[256,1152]{1,0:T(8,128)S(1)}, f32[256,1152]{1,0:T(8,128)S(1)}) custom-call(f32[1,1]{1,0:T(1,128)} %bitcast.13.refs_0_, f32[1,1]{1,0:T(1,128)} %bitcast.22.refs_1_, bf16[256,1152]{1,0:T(8,128)(2,1)S(1)} %get-tuple-element.51.refs_2_.img_n_ref, ...), custom_call_target="tpu_custom_call", output_to_operand_aliasing={{0}: (6, {}), {1}: (7, {})} | custom-call | flops 1000000000 | bytes 8388608 | tf_op jit(solution)/shard_map/pair/pallas_call | solution.py:136
  121.0 4.8 %last.1 = (f32[256,1152]{1,0:T(8,128)}, f32[256,1152]{1,0:T(8,128)}) custom-call(f32[1,1]{1,0:T(1,128)} %bitcast.14.temp_ref, f32[1,1]{1,0:T(1,128)} %bitcast.23.bias_ref, bf16[256,1152]{1,0:T(8,128)(2,1)S(1)} %get-tuple-element.51.refs_2_.img_n_ref, bf16[256,1152]{1,0:T(8,128)(2,1)S(1)} %get-tuple-element.52.refs_3_.txt_n_ref, ...), custom_call_target="tpu_custom_call" | custom-call | flops 2000000000 | bytes 8388608 | tf_op jit(solution)/shard_map/last/pallas_call | solution.py:179
  125.9 3.3 %all-to-all-done.1.parts_ref = f32[32,24,128]{2,1,0:T(8,128)} async-done(((f32[32,24,128]{2,1,0:T(8,128)}), f32[32,24,128]{2,1,0:T(8,128)}, u32[]{:S(2)}, u32[]{:S(2)}) %all-to-all-start.1) | async-done | bytes 393248 | tf_op jit(solution)/shard_map/all_to_all | solution.py:218
  129.1 1.7 %finish.1 = (f32[1,1]{1,0:T(1,128)}, f32[1,1]{1,0:T(1,128)}, f32[1,1]{1,0:T(1,128)}) custom-call(f32[32,24,128]{2,1,0:T(8,128)} %all-to-all-done.1.parts_ref), custom_call_target="tpu_custom_call" | custom-call | tf_op jit(solution)/shard_map/finish/pallas_call | solution.py:208
  (24 shorter events, 4.6 us)
Async XLA Ops:
  0.6 30.7 %collective-permute-start.3 = (bf16[256,1152]{1,0:T(8,128)(2,1)}, bf16[256,1152]{1,0:T(8,128)(2,1)S(1)}, u32[]{:S(2)}, u32[]{:S(2)}) collective-permute-start(bf16[256,1152]{1,0:T(8,128)(2,1)} %img_ref.3), channel_id=1, source_target_pairs={{0,496},{16,0},{32,16},{48,32},{64,48},{80,64},{96,80},{112,96},{1... | collective-permute-start | bytes 1769480 | tf_op jit(solution)/shard_map/ppermute | solution.py:16
  15.2 19.9 %collective-permute-start.2 = (bf16[256,1152]{1,0:T(8,128)(2,1)}, bf16[256,1152]{1,0:T(8,128)(2,1)S(1)}, u32[]{:S(2)}, u32[]{:S(2)}) collective-permute-start(bf16[256,1152]{1,0:T(8,128)(2,1)} %txt_ref.3), channel_id=1, source_target_pairs={{0,16},{16,32},{32,48},{48,64},{64,80},{80,96},{96,112},{112,128},... | collective-permute-start | bytes 1769480 | tf_op jit(solution)/shard_map/ppermute | solution.py:16
  17.1 30.6 %collective-permute-start = (bf16[256,1152]{1,0:T(8,128)(2,1)}, bf16[256,1152]{1,0:T(8,128)(2,1)S(1)}, u32[]{:S(2)}, u32[]{:S(2)}) collective-permute-start(bf16[256,1152]{1,0:T(8,128)(2,1)} %img_ref.3), channel_id=1, source_target_pairs={{0,16},{16,32},{32,48},{48,64},{64,80},{80,96},{96,112},{112,128},... | collective-permute-start | bytes 1769480 | tf_op jit(solution)/shard_map/ppermute | solution.py:16
  19.0 28.7 %collective-permute-start.1 = (bf16[256,1152]{1,0:T(8,128)(2,1)}, bf16[256,1152]{1,0:T(8,128)(2,1)S(1)}, u32[]{:S(2)}, u32[]{:S(2)}) collective-permute-start(bf16[256,1152]{1,0:T(8,128)(2,1)} %txt_ref.3), channel_id=1, source_target_pairs={{0,496},{16,0},{32,16},{48,32},{64,48},{80,64},{96,80},{112,96},{1... | collective-permute-start | bytes 1769480 | tf_op jit(solution)/shard_map/ppermute | solution.py:16
  27.6 1.1 copy-start.2
  28.7 1.1 copy-start.4
  35.1 25.4 %collective-permute-start.6 = (bf16[256,1152]{1,0:T(8,128)(2,1)S(1)}, bf16[256,1152]{1,0:T(8,128)(2,1)}, u32[]{:S(2)}, u32[]{:S(2)}) collective-permute-start(bf16[256,1152]{1,0:T(8,128)(2,1)S(1)} %collective-permute-done.2.refs_4_), channel_id=1, source_target_pairs={{0,16},{16,32},{32,48},{48,64},{64,80},{80,96},{96,112},{112,128},... | collective-permute-start | bytes 1769480 | tf_op jit(solution)/shard_map/ppermute | solution.py:16
  37.0 23.5 %collective-permute-start.7 = (bf16[256,1152]{1,0:T(8,128)(2,1)S(1)}, bf16[256,1152]{1,0:T(8,128)(2,1)}, u32[]{:S(2)}, u32[]{:S(2)}) collective-permute-start(bf16[256,1152]{1,0:T(8,128)(2,1)S(1)} %collective-permute-done.3.refs_5_), channel_id=1, source_target_pairs={{0,496},{16,0},{32,16},{48,32},{64,48},{80,64},{96,80},{112,96},{1... | collective-permute-start | bytes 1769480 | tf_op jit(solution)/shard_map/ppermute | solution.py:16
  47.7 25.4 %collective-permute-start.4 = (bf16[256,1152]{1,0:T(8,128)(2,1)S(1)}, bf16[256,1152]{1,0:T(8,128)(2,1)}, u32[]{:S(2)}, u32[]{:S(2)}) collective-permute-start(bf16[256,1152]{1,0:T(8,128)(2,1)S(1)} %collective-permute-done.refs_5_), channel_id=1, source_target_pairs={{0,16},{16,32},{32,48},{48,64},{64,80},{80,96},{96,112},{112,128},... | collective-permute-start | bytes 1769480 | tf_op jit(solution)/shard_map/ppermute | solution.py:16
  49.6 23.5 %collective-permute-start.5 = (bf16[256,1152]{1,0:T(8,128)(2,1)S(1)}, bf16[256,1152]{1,0:T(8,128)(2,1)}, u32[]{:S(2)}, u32[]{:S(2)}) collective-permute-start(bf16[256,1152]{1,0:T(8,128)(2,1)S(1)} %collective-permute-done.1.refs_4_), channel_id=1, source_target_pairs={{0,496},{16,0},{32,16},{48,32},{64,48},{80,64},{96,80},{112,96},{1... | collective-permute-start | bytes 1769480 | tf_op jit(solution)/shard_map/ppermute | solution.py:16
  60.5 36.9 %collective-permute-start.12 = (bf16[256,1152]{1,0:T(8,128)(2,1)}, bf16[256,1152]{1,0:T(8,128)(2,1)}, u32[]{:S(2)}, u32[]{:S(2)}) collective-permute-start(bf16[256,1152]{1,0:T(8,128)(2,1)} %collective-permute-done.7.refs_5_.i_ref), channel_id=1, source_target_pairs={{0,496},{16,0},{32,16},{48,32},{64,48},{80,64},{96,80},{112,96},{1... | collective-permute-start | bytes 1769480 | tf_op jit(solution)/shard_map/ppermute | solution.py:16
  62.4 37.3 %collective-permute-start.10 = (bf16[256,1152]{1,0:T(8,128)(2,1)}, bf16[256,1152]{1,0:T(8,128)(2,1)}, u32[]{:S(2)}, u32[]{:S(2)}) collective-permute-start(bf16[256,1152]{1,0:T(8,128)(2,1)} %collective-permute-done.6.refs_4_.t_ref), channel_id=1, source_target_pairs={{0,16},{16,32},{32,48},{48,64},{64,80},{80,96},{96,112},{112,128},... | collective-permute-start | bytes 1769480 | tf_op jit(solution)/shard_map/ppermute | solution.py:16
  73.1 34.9 %collective-permute-start.8 = (bf16[256,1152]{1,0:T(8,128)(2,1)}, bf16[256,1152]{1,0:T(8,128)(2,1)}, u32[]{:S(2)}, u32[]{:S(2)}) collective-permute-start(bf16[256,1152]{1,0:T(8,128)(2,1)} %collective-permute-done.4.refs_5_), channel_id=1, source_target_pairs={{0,16},{16,32},{32,48},{48,64},{64,80},{80,96},{96,112},{112,128},... | collective-permute-start | bytes 1769480 | tf_op jit(solution)/shard_map/ppermute | solution.py:16
  75.0 33.0 %collective-permute-start.9 = (bf16[256,1152]{1,0:T(8,128)(2,1)}, bf16[256,1152]{1,0:T(8,128)(2,1)}, u32[]{:S(2)}, u32[]{:S(2)}) collective-permute-start(bf16[256,1152]{1,0:T(8,128)(2,1)} %collective-permute-done.5.refs_4_), channel_id=1, source_target_pairs={{0,496},{16,0},{32,16},{48,32},{64,48},{80,64},{96,80},{112,96},{1... | collective-permute-start | bytes 1769480 | tf_op jit(solution)/shard_map/ppermute | solution.py:16
  85.9 0.7 copy-start.1
  86.5 21.5 %all-to-all-start = ((f32[16,24,128]{2,1,0:T(8,128)}), f32[16,24,128]{2,1,0:T(8,128)}, u32[]{:S(2)}, u32[]{:S(2)}) async-start(f32[16,24,128]{2,1,0:T(8,128)} %copy-done.1), calls=%async_computation | async-start | bytes 393216 | tf_op jit(solution)/shard_map/all_to_all | solution.py:218
  97.3 23.7 %collective-permute-start.13 = (bf16[256,1152]{1,0:T(8,128)(2,1)}, bf16[256,1152]{1,0:T(8,128)(2,1)}, u32[]{:S(2)}, u32[]{:S(2)}) collective-permute-start(bf16[256,1152]{1,0:T(8,128)(2,1)} %collective-permute-done.12.refs_5_), channel_id=1, source_target_pairs={{0,496},{16,0},{32,16},{48,32},{64,48},{80,64},{96,80},{112,96},{1... | collective-permute-start | bytes 1769480 | tf_op jit(solution)/shard_map/ppermute | solution.py:16
  99.7 21.3 %collective-permute-start.11 = (bf16[256,1152]{1,0:T(8,128)(2,1)}, bf16[256,1152]{1,0:T(8,128)(2,1)}, u32[]{:S(2)}, u32[]{:S(2)}) collective-permute-start(bf16[256,1152]{1,0:T(8,128)(2,1)} %collective-permute-done.10.refs_4_), channel_id=1, source_target_pairs={{0,16},{16,32},{32,48},{48,64},{64,80},{80,96},{96,112},{112,128},... | collective-permute-start | bytes 1769480 | tf_op jit(solution)/shard_map/ppermute | solution.py:16
  109.0 0.7 copy-start
  109.7 19.4 %all-to-all-start.1 = ((f32[32,24,128]{2,1,0:T(8,128)}), f32[32,24,128]{2,1,0:T(8,128)}, u32[]{:S(2)}, u32[]{:S(2)}) async-start(f32[32,24,128]{2,1,0:T(8,128)} %copy-done), calls=%async_computation.1 | async-start | bytes 786432 | tf_op jit(solution)/shard_map/all_to_all | solution.py:218
  117.7 3.3 %copy-start.3 = (bf16[256,1152]{1,0:T(8,128)(2,1)S(1)}, bf16[256,1152]{1,0:T(8,128)(2,1)}, u32[]{:S(2)}) copy-start(bf16[256,1152]{1,0:T(8,128)(2,1)} %img_ref.3) | copy-start | bytes 1769476
  117.7 3.3 %copy-start.5 = (bf16[256,1152]{1,0:T(8,128)(2,1)S(1)}, bf16[256,1152]{1,0:T(8,128)(2,1)}, u32[]{:S(2)}) copy-start(bf16[256,1152]{1,0:T(8,128)(2,1)} %txt_ref.3) | copy-start | bytes 1769476

commit v3 on v2

--- a/solution.py
+++ b/solution.py
@@ -8,7 +8,7 @@
 from jax.sharding import PartitionSpec as P
 
 F32, BF16 = jnp.float32, jnp.bfloat16
-COST_LAST, COST_PAIR = 2 * 10**9, 10**9
+COST_LAST, COST_PAIR, COST_FINISH = 2 * 10**9, 10**9, 115 * 10**9
 
 
 def shifted(array, by):
@@ -91,7 +91,7 @@
     )(temp, bias, image, text)
 
 
-def pair_kernel(with_older, counted, keep, *refs):
+def pair_kernel(with_older, crossed, counted, keep, *refs):
     refs = list(refs)
     temp_ref, bias_ref, img_n_ref, txt_n_ref, t_ref, i_ref, gimg_in, gtxt_in = refs[:8]
     del refs[:8]
@@ -118,9 +118,11 @@
     gtxt_ref[...] = gtxt_in[...] + jnp.dot(g, i_n, preferred_element_type=F32)
     if older is not None:
         off_diagonal(older[...], t_n, temp, bias, sums_ref)
-
-
-def pair(temp, bias, own, t, i, acc, sums=None, older=None, keep=False):
+    if crossed:
+        off_diagonal(i_n, t_n, temp, bias, sums_ref)
+
+
+def pair(temp, bias, own, t, i, acc, sums=None, older=None, crossed=False, keep=False):
     block = t.shape
     args = [temp, bias, *own, t, i, *acc]
     outs = [jax.ShapeDtypeStruct(block, F32)] * 2
@@ -134,31 +136,13 @@
     if keep:
         outs.append(jax.ShapeDtypeStruct(block, BF16))
     return pl.pallas_call(
-        functools.partial(pair_kernel, older is not None, sums is not None, keep),
+        functools.partial(pair_kernel, older is not None, crossed, sums is not None, keep),
         out_shape=tuple(outs),
         input_output_aliases=aliases,
         compiler_params=pltpu.CompilerParams(vmem_limit_bytes=24 << 20),
         cost_estimate=cost(COST_PAIR),
         name="pair",
     )(*args)
-
-
-def count_kernel(temp_ref, bias_ref, i_ref, t_ref, sums_in, sums_ref):
-    temp, bias = jnp.exp(temp_ref[...]), bias_ref[...]
-    sums_ref[...] = sums_in[...]
-    i_n = normal(i_ref[...])[0].astype(BF16)
-    t_n = normal(t_ref[...])[0].astype(BF16)
-    off_diagonal(i_n, t_n, temp, bias, sums_ref)
-
-
-def count(temp, bias, i, t, sums):
-    return pl.pallas_call(
-        count_kernel,
-        out_shape=jax.ShapeDtypeStruct((24, 128), F32),
-        input_output_aliases={4: 0},
-        compiler_params=pltpu.CompilerParams(vmem_limit_bytes=24 << 20),
-        name="count",
-    )(temp, bias, i, t, sums)
 
 
 def last_kernel(temp_ref, bias_ref, img_n_ref, txt_n_ref, t_ref, i_ref, gimg_in, gtxt_in, img_ref, txt_ref, gimg_ref, gtxt_ref):
@@ -209,6 +193,7 @@
         functools.partial(finish_kernel, pair_count),
         out_shape=(jax.ShapeDtypeStruct((1, 1), F32),) * 3,
         compiler_params=pltpu.CompilerParams(vmem_limit_bytes=8 << 20),
+        cost_estimate=cost(COST_FINISH),
         name="finish",
     )(parts)
     return tuple(total.reshape(1) for total in totals)
@@ -224,22 +209,26 @@
     after = lax.optimization_barrier
     t, i = {0: text}, {0: image}
     t[1], i[-1] = shifted(text, 1), shifted(image, -1)
-    i[1], t[-1] = shifted(image, 1), shifted(text, -1)
+    t[-1], i[1] = shifted(text, -1), shifted(image, 1)
     img_n, txt_n, *acc, sums = own_tile(temp, shift, image, text)
-    t[1], i[-1], img_n, txt_n = after((t[1], i[-1], img_n, txt_n))
+    t[1], img_n, txt_n = after((t[1], img_n, txt_n))
     own = (img_n, txt_n)
-    t[2], i[-2] = shifted(t[1], 1), shifted(i[-1], -1)
+    t[2] = shifted(t[1], 1)
     *acc, sums, i_m1 = pair(temp, shift, own, t[1], i[-1], acc, sums, keep=True)
-    i[1], t[-1], sums = after((i[1], t[-1], sums))
-    i[2], t[-2] = shifted(i[1], 1), shifted(t[-1], -1)
+    i[-1], sums = after((i[-1], sums))
+    i[-2] = shifted(i[-1], -1)
+    t[-2] = shifted(t[-1], -1)
     *acc, sums, i_1 = pair(temp, shift, own, t[-1], i[1], acc, sums, keep=True)
-    t[2], i[-2], sums = after((t[2], i[-2], sums))
-    t[3], i[-3] = shifted(t[2], 1), shifted(i[-2], -1)
-    *acc, sums = pair(temp, shift, own, t[2], i[-2], acc, sums, older=i_m1)
-    sums = count(temp, shift, i[-2], t[2], sums)
-    i[2], t[-2], sums = after((i[2], t[-2], sums))
-    i[3], t[-3] = shifted(i[2], 1), shifted(t[-2], -1)
+    i[1], sums = after((i[1], sums))
+    i[2] = shifted(i[1], 1)
+    t[3] = shifted(t[2], 1)
+    *acc, sums = pair(temp, shift, own, t[2], i[-2], acc, sums, older=i_m1, crossed=True)
+    i[-2], sums = after((i[-2], sums))
+    i[-3] = shifted(i[-2], -1)
+    t[-3] = shifted(t[-2], -1)
     *acc, sums = pair(temp, shift, own, t[-2], i[2], acc, sums, older=i_1)
+    i[2], sums = after((i[2], sums))
+    i[3] = shifted(i[2], 1)
     parts = to_all(spread(sums[None], lax.axis_size("dp")), "dp")
     t[4], i[-4] = shifted(t[3], 1), shifted(i[-3], -1)
     i[3], t[-3], parts = after((i[3], t[-3], parts))

time: 133 us -> 131 us (0.985)
  starting transfers between devices: 79.3 us -> 83.2 us
  waiting for transfers between devices: 17 us -> 13.7 us
  Pallas kernels: 28.8 us -> 27.1 us
    all_to_all x2, starting transfers between devices: 15.5 us -> 17.9 us  [to_all(): return lax.all_to_all(parts, axis, 0, 0)]
    ppermute x14, waiting for transfers between devices: 8.31 us -> 6.37 us  [shifted(): lax.ppermute(array, 'blk', [(i, (i + by) % length) for i in range(length)])]
    pallas_call x7 -> x6, Pallas kernels: 19.8 us -> 18.1 us  [pair(): pl.pallas_call(functools.partial(pair_kernel, older is not None, crossed,...]
    ppermute x14, starting transfers between devices: 63.8 us -> 65.3 us  [shifted(): lax.ppermute(array, 'blk', [(i, (i + by) % length) for i in range(length)])]
    all_to_all x2, waiting for transfers between devices: 8.64 us -> 7.31 us  [to_all(): return lax.all_to_all(parts, axis, 0, 0)]
  transfers between devices with their start and end apart: 16 -> 16, of which waited for: 6 -> 7; matrix products, arithmetic and copies ran while one was open for 0% -> 0% of each run, Pallas kernels for 21% -> 20%
where the time goes in v3:
time: 131 us; the launch traced here: 130 us
  starting transfers between devices  83.2 us (64%)
  Pallas kernels  27.1 us (21%)
  waiting for transfers between devices  13.7 us (10%)
  local copies, waits for them, and re-layouts  3.54 us (3%)
  between operations  2.18 us (2%)
    ppermute x14, starting transfers between devices, shifted(): lax.ppermute(array, 'blk', [(i, (i + by) % length) for i in range(length)])  65.3 us
    pallas_call x6, Pallas kernels, pair(): pl.pallas_call(functools.partial(pair_kernel, older is not None, crossed,...  18.1 us
    all_to_all x2, starting transfers between devices, to_all(): return lax.all_to_all(parts, axis, 0, 0)  17.9 us
    all_to_all x2, waiting for transfers between devices, to_all(): return lax.all_to_all(parts, axis, 0, 0)  7.31 us
    ppermute x14, waiting for transfers between devices, shifted(): lax.ppermute(array, 'blk', [(i, (i + by) % length) for i in range(length)])  6.37 us
    pallas_call x1, Pallas kernels, last(): pl.pallas_call(last_kernel, out_shape=(jax.ShapeDtypeStruct(block, F32),)...  4.83 us
    unnamed x12, local copies, waits for them, and re-layouts  3.54 us
  transfers between devices with their start and end apart: 16, of which 7 were waited for; matrix products, arithmetic and copies ran while one was open for 0% of the time, Pallas kernels for 20%

profile of v3, /device:TPU:1, one launch (start us, length us, event | category | flops | bytes accessed | tf_op | source)
XLA Modules:
  0.0 129.7 jit_solution(14684834439540304531)
XLA Ops:
  0.6 4.8 %collective-permute-start.1 = (bf16[256,1152]{1,0:T(8,128)(2,1)}, bf16[256,1152]{1,0:T(8,128)(2,1)S(1)}, u32[]{:S(2)}, u32[]{:S(2)}) collective-permute-start(bf16[256,1152]{1,0:T(8,128)(2,1)} %txt_ref.3), channel_id=1, source_target_pairs={{0,16},{16,32},{32,48},{48,64},{64,80},{80,96},{96,112},{112,128},... | collective-permute-start | bytes 1769480 | tf_op jit(solution)/shard_map/ppermute | solution.py:16
  5.5 11.6 %collective-permute-start.3 = (bf16[256,1152]{1,0:T(8,128)(2,1)}, bf16[256,1152]{1,0:T(8,128)(2,1)S(1)}, u32[]{:S(2)}, u32[]{:S(2)}) collective-permute-start(bf16[256,1152]{1,0:T(8,128)(2,1)} %img_ref.3), channel_id=1, source_target_pairs={{0,496},{16,0},{32,16},{48,32},{64,48},{80,64},{96,80},{112,96},{1... | collective-permute-start | bytes 1769480 | tf_op jit(solution)/shard_map/ppermute | solution.py:16
  17.1 1.9 %collective-permute-start = (bf16[256,1152]{1,0:T(8,128)(2,1)}, bf16[256,1152]{1,0:T(8,128)(2,1)S(1)}, u32[]{:S(2)}, u32[]{:S(2)}) collective-permute-start(bf16[256,1152]{1,0:T(8,128)(2,1)} %img_ref.3), channel_id=1, source_target_pairs={{0,16},{16,32},{32,48},{48,64},{64,80},{80,96},{96,112},{112,128},... | collective-permute-start | bytes 1769480 | tf_op jit(solution)/shard_map/ppermute | solution.py:16
  19.0 7.3 %collective-permute-start.2 = (bf16[256,1152]{1,0:T(8,128)(2,1)}, bf16[256,1152]{1,0:T(8,128)(2,1)S(1)}, u32[]{:S(2)}, u32[]{:S(2)}) collective-permute-start(bf16[256,1152]{1,0:T(8,128)(2,1)} %txt_ref.3), channel_id=1, source_target_pairs={{0,496},{16,0},{32,16},{48,32},{64,48},{80,64},{96,80},{112,96},{1... | collective-permute-start | bytes 1769480 | tf_op jit(solution)/shard_map/ppermute | solution.py:16
  27.6 1.1 copy-done.2
  28.7 1.1 copy-done.4
  29.7 1.6 %own_tile.1 = (bf16[256,1152]{1,0:T(8,128)(2,1)S(1)}, bf16[256,1152]{1,0:T(8,128)(2,1)S(1)}, f32[256,1152]{1,0:T(8,128)S(1)}, f32[256,1152]{1,0:T(8,128)S(1)}, f32[24,128]{1,0:T(8,128)S(1)}) custom-call(f32[1,1]{1,0:T(1,128)} %bitcast.6.temp_ref, f32[1,1]{1,0:T(1,128)} %bitcast.14.bias_ref, bf16[256,1152]{1,0:T(8,128)(2,1)S(1)} %copy-done.2, ...), custom_call_target="tpu_custom_call" | custom-call | tf_op jit(solution)/shard_map/own_tile/pallas_call | solution.py:80
  31.3 2.1 %pair.6 = (f32[256,1152]{1,0:T(8,128)S(1)}, f32[256,1152]{1,0:T(8,128)S(1)}, f32[24,128]{1,0:T(8,128)S(1)}, bf16[256,1152]{1,0:T(8,128)(2,1)S(1)}) custom-call(f32[1,1]{1,0:T(1,128)} %bitcast.7.refs_0_, f32[1,1]{1,0:T(1,128)} %bitcast.15.refs_1_, ...), custom_call_target="tpu_custom_call", output_to_operand_aliasing={{0}: (6, {}), {1}: (7, {}), {2}: (8, {})} | custom-call | flops 1000000000 | bytes 8388608 | tf_op jit(solution)/shard_map/pair/pallas_call | solution.py:138
  33.4 6.0 %collective-permute-start.7 = (bf16[256,1152]{1,0:T(8,128)(2,1)S(1)}, bf16[256,1152]{1,0:T(8,128)(2,1)}, u32[]{:S(2)}, u32[]{:S(2)}) collective-permute-start(bf16[256,1152]{1,0:T(8,128)(2,1)S(1)} %collective-permute-done.3.refs_5_), channel_id=1, source_target_pairs={{0,496},{16,0},{32,16},{48,32},{64,48},{80,64},{96,80},{112,96},{1... | collective-permute-start | bytes 1769480 | tf_op jit(solution)/shard_map/ppermute | solution.py:16
  39.4 1.9 %collective-permute-start.6 = (bf16[256,1152]{1,0:T(8,128)(2,1)S(1)}, bf16[256,1152]{1,0:T(8,128)(2,1)}, u32[]{:S(2)}, u32[]{:S(2)}) collective-permute-start(bf16[256,1152]{1,0:T(8,128)(2,1)S(1)} %collective-permute-done.1.refs_4_), channel_id=1, source_target_pairs={{0,16},{16,32},{32,48},{48,64},{64,80},{80,96},{96,112},{112,128},... | collective-permute-start | bytes 1769480 | tf_op jit(solution)/shard_map/ppermute | solution.py:16
  42.0 2.1 %pair.7 = (f32[256,1152]{1,0:T(8,128)S(1)}, f32[256,1152]{1,0:T(8,128)S(1)}, f32[24,128]{1,0:T(8,128)S(1)}, bf16[256,1152]{1,0:T(8,128)(2,1)S(1)}) custom-call(f32[1,1]{1,0:T(1,128)} %bitcast.8.refs_0_, f32[1,1]{1,0:T(1,128)} %bitcast.16.refs_1_, ...), custom_call_target="tpu_custom_call", output_to_operand_aliasing={{0}: (6, {}), {1}: (7, {}), {2}: (8, {})} | custom-call | flops 1000000000 | bytes 8388608 | tf_op jit(solution)/shard_map/pair/pallas_call | solution.py:138
  44.1 1.9 %collective-permute-start.4 = (bf16[256,1152]{1,0:T(8,128)(2,1)S(1)}, bf16[256,1152]{1,0:T(8,128)(2,1)}, u32[]{:S(2)}, u32[]{:S(2)}) collective-permute-start(bf16[256,1152]{1,0:T(8,128)(2,1)S(1)} %collective-permute-done.refs_5_), channel_id=1, source_target_pairs={{0,16},{16,32},{32,48},{48,64},{64,80},{80,96},{96,112},{112,128},... | collective-permute-start | bytes 1769480 | tf_op jit(solution)/shard_map/ppermute | solution.py:16
  46.1 7.9 %collective-permute-start.5 = (bf16[256,1152]{1,0:T(8,128)(2,1)S(1)}, bf16[256,1152]{1,0:T(8,128)(2,1)}, u32[]{:S(2)}, u32[]{:S(2)}) collective-permute-start(bf16[256,1152]{1,0:T(8,128)(2,1)S(1)} %collective-permute-done.2.refs_4_), channel_id=1, source_target_pairs={{0,496},{16,0},{32,16},{48,32},{64,48},{80,64},{96,80},{112,96},{1... | collective-permute-start | bytes 1769480 | tf_op jit(solution)/shard_map/ppermute | solution.py:16
  54.6 2.6 %collective-permute-done.6.refs_4_ = bf16[256,1152]{1,0:T(8,128)(2,1)} collective-permute-done((bf16[256,1152]{1,0:T(8,128)(2,1)S(1)}, bf16[256,1152]{1,0:T(8,128)(2,1)}, u32[]{:S(2)}, u32[]{:S(2)}) %collective-permute-start.6) | collective-permute-done | bytes 589856 | tf_op jit(solution)/shard_map/ppermute | solution.py:16
  57.2 3.9 %pair.8 = (f32[256,1152]{1,0:T(8,128)S(1)}, f32[256,1152]{1,0:T(8,128)S(1)}, f32[24,128]{1,0:T(8,128)S(1)}) custom-call(f32[1,1]{1,0:T(1,128)} %bitcast.9.refs_0_, f32[1,1]{1,0:T(1,128)} %bitcast.17.refs_1_, bf16[256,1152]{1,0:T(8,128)(2,1)S(1)} %get-tuple-element.49.refs_2_.img_n_ref, ...), custom_call_target="tpu_custom_call", output_to_operand_aliasing={{0}: (6, {}), {1}: (7, {}), {2}: (9, {})} | custom-call | flops 1000000000 | bytes 8388608 | tf_op jit(solution)/shard_map/pair/pallas_call | solution.py:138
  61.1 5.5 %collective-permute-start.12 = (bf16[256,1152]{1,0:T(8,128)(2,1)}, bf16[256,1152]{1,0:T(8,128)(2,1)}, u32[]{:S(2)}, u32[]{:S(2)}) collective-permute-start(bf16[256,1152]{1,0:T(8,128)(2,1)} %collective-permute-done.7.refs_5_), channel_id=1, source_target_pairs={{0,496},{16,0},{32,16},{48,32},{64,48},{80,64},{96,80},{112,96},{1... | collective-permute-start | bytes 1769480 | tf_op jit(solution)/shard_map/ppermute | solution.py:16
  66.6 1.9 %collective-permute-start.10 = (bf16[256,1152]{1,0:T(8,128)(2,1)}, bf16[256,1152]{1,0:T(8,128)(2,1)}, u32[]{:S(2)}, u32[]{:S(2)}) collective-permute-start(bf16[256,1152]{1,0:T(8,128)(2,1)} %collective-permute-done.6.refs_4_), channel_id=1, source_target_pairs={{0,16},{16,32},{32,48},{48,64},{64,80},{80,96},{96,112},{112,128},... | collective-permute-start | bytes 1769480 | tf_op jit(solution)/shard_map/ppermute | solution.py:16
  68.5 1.3 %collective-permute-done.4.refs_5_ = bf16[256,1152]{1,0:T(8,128)(2,1)} collective-permute-done((bf16[256,1152]{1,0:T(8,128)(2,1)S(1)}, bf16[256,1152]{1,0:T(8,128)(2,1)}, u32[]{:S(2)}, u32[]{:S(2)}) %collective-permute-start.4) | collective-permute-done | bytes 589856 | tf_op jit(solution)/shard_map/ppermute | solution.py:16
  69.8 3.5 %pair.9 = (f32[256,1152]{1,0:T(8,128)S(1)}, f32[256,1152]{1,0:T(8,128)S(1)}, f32[24,128]{1,0:T(8,128)S(1)}) custom-call(f32[1,1]{1,0:T(1,128)} %bitcast.10.refs_0_, f32[1,1]{1,0:T(1,128)} %bitcast.18.refs_1_, bf16[256,1152]{1,0:T(8,128)(2,1)S(1)} %get-tuple-element.49.refs_2_.img_n_ref, ...), custom_call_target="tpu_custom_call", output_to_operand_aliasing={{0}: (6, {}), {1}: (7, {}), {2}: (9, {})} | custom-call | flops 1000000000 | bytes 8388608 | tf_op jit(solution)/shard_map/pair/pallas_call | solution.py:138
  73.4 1.9 %collective-permute-start.8 = (bf16[256,1152]{1,0:T(8,128)(2,1)}, bf16[256,1152]{1,0:T(8,128)(2,1)}, u32[]{:S(2)}, u32[]{:S(2)}) collective-permute-start(bf16[256,1152]{1,0:T(8,128)(2,1)} %collective-permute-done.4.refs_5_), channel_id=1, source_target_pairs={{0,16},{16,32},{32,48},{48,64},{64,80},{80,96},{96,112},{112,128},... | collective-permute-start | bytes 1769480 | tf_op jit(solution)/shard_map/ppermute | solution.py:16
  75.3 7.3 %collective-permute-start.9 = (bf16[256,1152]{1,0:T(8,128)(2,1)}, bf16[256,1152]{1,0:T(8,128)(2,1)}, u32[]{:S(2)}, u32[]{:S(2)}) collective-permute-start(bf16[256,1152]{1,0:T(8,128)(2,1)} %collective-permute-done.5.refs_4_), channel_id=1, source_target_pairs={{0,496},{16,0},{32,16},{48,32},{64,48},{80,64},{96,80},{112,96},{1... | collective-permute-start | bytes 1769480 | tf_op jit(solution)/shard_map/ppermute | solution.py:16
  83.3 11.9 %all-to-all-start = ((f32[16,24,128]{2,1,0:T(8,128)}), f32[16,24,128]{2,1,0:T(8,128)}, u32[]{:S(2)}, u32[]{:S(2)}) async-start(f32[16,24,128]{2,1,0:T(8,128)} %copy-done.1), calls=%async_computation | async-start | bytes 393216 | tf_op jit(solution)/shard_map/all_to_all | solution.py:203
  95.2 1.9 %collective-permute-start.13 = (bf16[256,1152]{1,0:T(8,128)(2,1)}, bf16[256,1152]{1,0:T(8,128)(2,1)}, u32[]{:S(2)}, u32[]{:S(2)}) collective-permute-start(bf16[256,1152]{1,0:T(8,128)(2,1)} %collective-permute-done.12.refs_5_), channel_id=1, source_target_pairs={{0,496},{16,0},{32,16},{48,32},{64,48},{80,64},{96,80},{112,96},{1... | collective-permute-start | bytes 1769480 | tf_op jit(solution)/shard_map/ppermute | solution.py:16
  97.2 3.4 %collective-permute-start.11 = (bf16[256,1152]{1,0:T(8,128)(2,1)}, bf16[256,1152]{1,0:T(8,128)(2,1)}, u32[]{:S(2)}, u32[]{:S(2)}) collective-permute-start(bf16[256,1152]{1,0:T(8,128)(2,1)} %collective-permute-done.10.refs_4_), channel_id=1, source_target_pairs={{0,16},{16,32},{32,48},{48,64},{64,80},{80,96},{96,112},{112,128},... | collective-permute-start | bytes 1769480 | tf_op jit(solution)/shard_map/ppermute | solution.py:16
  100.5 5.4 %all-to-all-done.parts_ref = f32[16,24,128]{2,1,0:T(8,128)} async-done(((f32[16,24,128]{2,1,0:T(8,128)}), f32[16,24,128]{2,1,0:T(8,128)}, u32[]{:S(2)}, u32[]{:S(2)}) %all-to-all-start) | async-done | bytes 196640 | tf_op jit(solution)/shard_map/all_to_all | solution.py:203
  107.6 6.0 %all-to-all-start.1 = ((f32[32,24,128]{2,1,0:T(8,128)}), f32[32,24,128]{2,1,0:T(8,128)}, u32[]{:S(2)}, u32[]{:S(2)}) async-start(f32[32,24,128]{2,1,0:T(8,128)} %copy-done), calls=%async_computation.1 | async-start | bytes 786432 | tf_op jit(solution)/shard_map/all_to_all | solution.py:203
  113.6 3.2 %pair.10 = (f32[256,1152]{1,0:T(8,128)S(1)}, f32[256,1152]{1,0:T(8,128)S(1)}) custom-call(f32[1,1]{1,0:T(1,128)} %bitcast.11.refs_0_, f32[1,1]{1,0:T(1,128)} %bitcast.19.refs_1_, bf16[256,1152]{1,0:T(8,128)(2,1)S(1)} %get-tuple-element.49.refs_2_.img_n_ref, ...), custom_call_target="tpu_custom_call", output_to_operand_aliasing={{0}: (6, {}), {1}: (7, {})} | custom-call | flops 1000000000 | bytes 8388608 | tf_op jit(solution)/shard_map/pair/pallas_call | solution.py:138
  116.8 3.3 %pair.11 = (f32[256,1152]{1,0:T(8,128)S(1)}, f32[256,1152]{1,0:T(8,128)S(1)}) custom-call(f32[1,1]{1,0:T(1,128)} %bitcast.12.refs_0_, f32[1,1]{1,0:T(1,128)} %bitcast.20.refs_1_, bf16[256,1152]{1,0:T(8,128)(2,1)S(1)} %get-tuple-element.49.refs_2_.img_n_ref, ...), custom_call_target="tpu_custom_call", output_to_operand_aliasing={{0}: (6, {}), {1}: (7, {})} | custom-call | flops 1000000000 | bytes 8388608 | tf_op jit(solution)/shard_map/pair/pallas_call | solution.py:138
  120.1 1.2 collective-permute-done.11.t_ref
  121.3 4.8 %last.1 = (f32[256,1152]{1,0:T(8,128)}, f32[256,1152]{1,0:T(8,128)}) custom-call(f32[1,1]{1,0:T(1,128)} %bitcast.13.temp_ref, f32[1,1]{1,0:T(1,128)} %bitcast.21.bias_ref, bf16[256,1152]{1,0:T(8,128)(2,1)S(1)} %get-tuple-element.49.refs_2_.img_n_ref, bf16[256,1152]{1,0:T(8,128)(2,1)S(1)} %get-tuple-element.50.refs_3_.txt_n_ref, ...), custom_call_target="tpu_custom_call" | custom-call | flops 2000000000 | bytes 8388608 | tf_op jit(solution)/shard_map/last/pallas_call | solution.py:163
  126.1 1.9 %all-to-all-done.1.parts_ref = f32[32,24,128]{2,1,0:T(8,128)} async-done(((f32[32,24,128]{2,1,0:T(8,128)}), f32[32,24,128]{2,1,0:T(8,128)}, u32[]{:S(2)}, u32[]{:S(2)}) %all-to-all-start.1) | async-done | bytes 393248 | tf_op jit(solution)/shard_map/all_to_all | solution.py:203
  128.1 1.7 %finish.1 = (f32[1,1]{1,0:T(1,128)}, f32[1,1]{1,0:T(1,128)}, f32[1,1]{1,0:T(1,128)}) custom-call(f32[32,24,128]{2,1,0:T(8,128)} %all-to-all-done.1.parts_ref), custom_call_target="tpu_custom_call" | custom-call | flops 115000000512 | bytes 8388608 | tf_op jit(solution)/shard_map/finish/pallas_call | solution.py:192
  (23 shorter events, 3.7 us)
Async XLA Ops:
  0.6 30.7 %collective-permute-start.1 = (bf16[256,1152]{1,0:T(8,128)(2,1)}, bf16[256,1152]{1,0:T(8,128)(2,1)S(1)}, u32[]{:S(2)}, u32[]{:S(2)}) collective-permute-start(bf16[256,1152]{1,0:T(8,128)(2,1)} %txt_ref.3), channel_id=1, source_target_pairs={{0,16},{16,32},{32,48},{48,64},{64,80},{80,96},{96,112},{112,128},... | collective-permute-start | bytes 1769480 | tf_op jit(solution)/shard_map/ppermute | solution.py:16
  5.5 25.8 %collective-permute-start.3 = (bf16[256,1152]{1,0:T(8,128)(2,1)}, bf16[256,1152]{1,0:T(8,128)(2,1)S(1)}, u32[]{:S(2)}, u32[]{:S(2)}) collective-permute-start(bf16[256,1152]{1,0:T(8,128)(2,1)} %img_ref.3), channel_id=1, source_target_pairs={{0,496},{16,0},{32,16},{48,32},{64,48},{80,64},{96,80},{112,96},{1... | collective-permute-start | bytes 1769480 | tf_op jit(solution)/shard_map/ppermute | solution.py:16
  17.1 24.3 %collective-permute-start = (bf16[256,1152]{1,0:T(8,128)(2,1)}, bf16[256,1152]{1,0:T(8,128)(2,1)S(1)}, u32[]{:S(2)}, u32[]{:S(2)}) collective-permute-start(bf16[256,1152]{1,0:T(8,128)(2,1)} %img_ref.3), channel_id=1, source_target_pairs={{0,16},{16,32},{32,48},{48,64},{64,80},{80,96},{96,112},{112,128},... | collective-permute-start | bytes 1769480 | tf_op jit(solution)/shard_map/ppermute | solution.py:16
  19.0 23.0 %collective-permute-start.2 = (bf16[256,1152]{1,0:T(8,128)(2,1)}, bf16[256,1152]{1,0:T(8,128)(2,1)S(1)}, u32[]{:S(2)}, u32[]{:S(2)}) collective-permute-start(bf16[256,1152]{1,0:T(8,128)(2,1)} %txt_ref.3), channel_id=1, source_target_pairs={{0,496},{16,0},{32,16},{48,32},{64,48},{80,64},{96,80},{112,96},{1... | collective-permute-start | bytes 1769480 | tf_op jit(solution)/shard_map/ppermute | solution.py:16
  27.6 1.1 copy-start.2
  28.7 1.1 copy-start.4
  33.4 21.1 %collective-permute-start.7 = (bf16[256,1152]{1,0:T(8,128)(2,1)S(1)}, bf16[256,1152]{1,0:T(8,128)(2,1)}, u32[]{:S(2)}, u32[]{:S(2)}) collective-permute-start(bf16[256,1152]{1,0:T(8,128)(2,1)S(1)} %collective-permute-done.3.refs_5_), channel_id=1, source_target_pairs={{0,496},{16,0},{32,16},{48,32},{64,48},{80,64},{96,80},{112,96},{1... | collective-permute-start | bytes 1769480 | tf_op jit(solution)/shard_map/ppermute | solution.py:16
  39.4 17.8 %collective-permute-start.6 = (bf16[256,1152]{1,0:T(8,128)(2,1)S(1)}, bf16[256,1152]{1,0:T(8,128)(2,1)}, u32[]{:S(2)}, u32[]{:S(2)}) collective-permute-start(bf16[256,1152]{1,0:T(8,128)(2,1)S(1)} %collective-permute-done.1.refs_4_), channel_id=1, source_target_pairs={{0,16},{16,32},{32,48},{48,64},{64,80},{80,96},{96,112},{112,128},... | collective-permute-start | bytes 1769480 | tf_op jit(solution)/shard_map/ppermute | solution.py:16
  44.1 25.7 %collective-permute-start.4 = (bf16[256,1152]{1,0:T(8,128)(2,1)S(1)}, bf16[256,1152]{1,0:T(8,128)(2,1)}, u32[]{:S(2)}, u32[]{:S(2)}) collective-permute-start(bf16[256,1152]{1,0:T(8,128)(2,1)S(1)} %collective-permute-done.refs_5_), channel_id=1, source_target_pairs={{0,16},{16,32},{32,48},{48,64},{64,80},{80,96},{96,112},{112,128},... | collective-permute-start | bytes 1769480 | tf_op jit(solution)/shard_map/ppermute | solution.py:16
  46.1 23.7 %collective-permute-start.5 = (bf16[256,1152]{1,0:T(8,128)(2,1)S(1)}, bf16[256,1152]{1,0:T(8,128)(2,1)}, u32[]{:S(2)}, u32[]{:S(2)}) collective-permute-start(bf16[256,1152]{1,0:T(8,128)(2,1)S(1)} %collective-permute-done.2.refs_4_), channel_id=1, source_target_pairs={{0,496},{16,0},{32,16},{48,32},{64,48},{80,64},{96,80},{112,96},{1... | collective-permute-start | bytes 1769480 | tf_op jit(solution)/shard_map/ppermute | solution.py:16
  61.1 34.2 %collective-permute-start.12 = (bf16[256,1152]{1,0:T(8,128)(2,1)}, bf16[256,1152]{1,0:T(8,128)(2,1)}, u32[]{:S(2)}, u32[]{:S(2)}) collective-permute-start(bf16[256,1152]{1,0:T(8,128)(2,1)} %collective-permute-done.7.refs_5_), channel_id=1, source_target_pairs={{0,496},{16,0},{32,16},{48,32},{64,48},{80,64},{96,80},{112,96},{1... | collective-permute-start | bytes 1769480 | tf_op jit(solution)/shard_map/ppermute | solution.py:16
  66.6 30.6 %collective-permute-start.10 = (bf16[256,1152]{1,0:T(8,128)(2,1)}, bf16[256,1152]{1,0:T(8,128)(2,1)}, u32[]{:S(2)}, u32[]{:S(2)}) collective-permute-start(bf16[256,1152]{1,0:T(8,128)(2,1)} %collective-permute-done.6.refs_4_), channel_id=1, source_target_pairs={{0,16},{16,32},{32,48},{48,64},{64,80},{80,96},{96,112},{112,128},... | collective-permute-start | bytes 1769480 | tf_op jit(solution)/shard_map/ppermute | solution.py:16
  73.4 32.5 %collective-permute-start.8 = (bf16[256,1152]{1,0:T(8,128)(2,1)}, bf16[256,1152]{1,0:T(8,128)(2,1)}, u32[]{:S(2)}, u32[]{:S(2)}) collective-permute-start(bf16[256,1152]{1,0:T(8,128)(2,1)} %collective-permute-done.4.refs_5_), channel_id=1, source_target_pairs={{0,16},{16,32},{32,48},{48,64},{64,80},{80,96},{96,112},{112,128},... | collective-permute-start | bytes 1769480 | tf_op jit(solution)/shard_map/ppermute | solution.py:16
  75.3 30.6 %collective-permute-start.9 = (bf16[256,1152]{1,0:T(8,128)(2,1)}, bf16[256,1152]{1,0:T(8,128)(2,1)}, u32[]{:S(2)}, u32[]{:S(2)}) collective-permute-start(bf16[256,1152]{1,0:T(8,128)(2,1)} %collective-permute-done.5.refs_4_), channel_id=1, source_target_pairs={{0,496},{16,0},{32,16},{48,32},{64,48},{80,64},{96,80},{112,96},{1... | collective-permute-start | bytes 1769480 | tf_op jit(solution)/shard_map/ppermute | solution.py:16
  82.6 0.7 copy-start.1
  83.3 22.6 %all-to-all-start = ((f32[16,24,128]{2,1,0:T(8,128)}), f32[16,24,128]{2,1,0:T(8,128)}, u32[]{:S(2)}, u32[]{:S(2)}) async-start(f32[16,24,128]{2,1,0:T(8,128)} %copy-done.1), calls=%async_computation | async-start | bytes 393216 | tf_op jit(solution)/shard_map/all_to_all | solution.py:203
  95.2 24.8 %collective-permute-start.13 = (bf16[256,1152]{1,0:T(8,128)(2,1)}, bf16[256,1152]{1,0:T(8,128)(2,1)}, u32[]{:S(2)}, u32[]{:S(2)}) collective-permute-start(bf16[256,1152]{1,0:T(8,128)(2,1)} %collective-permute-done.12.refs_5_), channel_id=1, source_target_pairs={{0,496},{16,0},{32,16},{48,32},{64,48},{80,64},{96,80},{112,96},{1... | collective-permute-start | bytes 1769480 | tf_op jit(solution)/shard_map/ppermute | solution.py:16
  97.2 24.1 %collective-permute-start.11 = (bf16[256,1152]{1,0:T(8,128)(2,1)}, bf16[256,1152]{1,0:T(8,128)(2,1)}, u32[]{:S(2)}, u32[]{:S(2)}) collective-permute-start(bf16[256,1152]{1,0:T(8,128)(2,1)} %collective-permute-done.10.refs_4_), channel_id=1, source_target_pairs={{0,16},{16,32},{32,48},{48,64},{64,80},{80,96},{96,112},{112,128},... | collective-permute-start | bytes 1769480 | tf_op jit(solution)/shard_map/ppermute | solution.py:16
  106.9 0.7 copy-start
  107.6 20.4 %all-to-all-start.1 = ((f32[32,24,128]{2,1,0:T(8,128)}), f32[32,24,128]{2,1,0:T(8,128)}, u32[]{:S(2)}, u32[]{:S(2)}) async-start(f32[32,24,128]{2,1,0:T(8,128)} %copy-done), calls=%async_computation.1 | async-start | bytes 786432 | tf_op jit(solution)/shard_map/all_to_all | solution.py:203
  116.8 4.5 %copy-start.3 = (bf16[256,1152]{1,0:T(8,128)(2,1)S(1)}, bf16[256,1152]{1,0:T(8,128)(2,1)}, u32[]{:S(2)}) copy-start(bf16[256,1152]{1,0:T(8,128)(2,1)} %img_ref.3) | copy-start | bytes 1769476
  116.8 4.5 %copy-start.5 = (bf16[256,1152]{1,0:T(8,128)(2,1)S(1)}, bf16[256,1152]{1,0:T(8,128)(2,1)}, u32[]{:S(2)}) copy-start(bf16[256,1152]{1,0:T(8,128)(2,1)} %txt_ref.3) | copy-start | bytes 1769476

commit v4 on v3

--- a/solution.py
+++ b/solution.py
@@ -231,9 +231,9 @@
     i[3] = shifted(i[2], 1)
     parts = to_all(spread(sums[None], lax.axis_size("dp")), "dp")
     t[4], i[-4] = shifted(t[3], 1), shifted(i[-3], -1)
-    i[3], t[-3], parts = after((i[3], t[-3], parts))
+    acc = pair(temp, shift, own, t[3], i[-3], acc)
+    acc, i[3], t[-3], parts = after((acc, i[3], t[-3], parts))
     parts = to_all(spread(parts, lax.axis_size("blk")), "blk")
-    acc = pair(temp, shift, own, t[3], i[-3], acc)
     acc = pair(temp, shift, own, t[-3], i[3], acc)
     grad_image, grad_text = last(temp, shift, own, t[4], i[-4], acc, image, text)
     return (*finish(parts, pair_count), grad_image, grad_text)

time: 131 us -> 131 us (level)
  starting transfers between devices: 83.2 us -> 81 us
  waiting for transfers between devices: 13.7 us -> 15.9 us
    ppermute x14, waiting for transfers between devices: 6.37 us -> 11.7 us  [shifted(): lax.ppermute(array, 'blk', [(i, (i + by) % length) for i in range(length)])]
    all_to_all x2, waiting for transfers between devices: 7.31 us -> 4.12 us  [to_all(): return lax.all_to_all(parts, axis, 0, 0)]
    ppermute x14, starting transfers between devices: 65.3 us -> 63.3 us  [shifted(): lax.ppermute(array, 'blk', [(i, (i + by) % length) for i in range(length)])]
  transfers between devices with their start and end apart: 16 -> 16, of which waited for: 7 -> 9; matrix products, arithmetic and copies ran while one was open for 0% -> 0% of each run, Pallas kernels for 20% -> 20%
where the time goes in v4:
time: 131 us; the launch traced here: 130 us
  starting transfers between devices  81 us (62%)
  Pallas kernels  27.1 us (21%)
  waiting for transfers between devices  15.9 us (12%)
  local copies, waits for them, and re-layouts  3.54 us (3%)
  between operations  2.16 us (2%)
    ppermute x14, starting transfers between devices, shifted(): lax.ppermute(array, 'blk', [(i, (i + by) % length) for i in range(length)])  63.3 us
    pallas_call x6, Pallas kernels, pair(): pl.pallas_call(functools.partial(pair_kernel, older is not None, crossed,...  18.1 us
    all_to_all x2, starting transfers between devices, to_all(): return lax.all_to_all(parts, axis, 0, 0)  17.7 us
    ppermute x14, waiting for transfers between devices, shifted(): lax.ppermute(array, 'blk', [(i, (i + by) % length) for i in range(length)])  11.7 us
    pallas_call x1, Pallas kernels, last(): pl.pallas_call(last_kernel, out_shape=(jax.ShapeDtypeStruct(block, F32),)...  4.83 us
    all_to_all x2, waiting for transfers between devices, to_all(): return lax.all_to_all(parts, axis, 0, 0)  4.12 us
    unnamed x12, local copies, waits for them, and re-layouts  3.54 us
  transfers between devices with their start and end apart: 16, of which 9 were waited for; matrix products, arithmetic and copies ran while one was open for 0% of the time, Pallas kernels for 20%

profile of v4, /device:TPU:1, one launch (start us, length us, event | category | flops | bytes accessed | tf_op | source)
XLA Modules:
  0.0 129.7 jit_solution(1404290344119206379)
XLA Ops:
  0.6 4.8 %collective-permute-start = (bf16[256,1152]{1,0:T(8,128)(2,1)}, bf16[256,1152]{1,0:T(8,128)(2,1)S(1)}, u32[]{:S(2)}, u32[]{:S(2)}) collective-permute-start(bf16[256,1152]{1,0:T(8,128)(2,1)} %txt_ref.3), channel_id=1, source_target_pairs={{0,16},{16,32},{32,48},{48,64},{64,80},{80,96},{96,112},{112,128},... | collective-permute-start | bytes 1769480 | tf_op jit(solution)/shard_map/ppermute | solution.py:16
  5.5 11.6 %collective-permute-start.3 = (bf16[256,1152]{1,0:T(8,128)(2,1)}, bf16[256,1152]{1,0:T(8,128)(2,1)S(1)}, u32[]{:S(2)}, u32[]{:S(2)}) collective-permute-start(bf16[256,1152]{1,0:T(8,128)(2,1)} %img_ref.3), channel_id=1, source_target_pairs={{0,496},{16,0},{32,16},{48,32},{64,48},{80,64},{96,80},{112,96},{1... | collective-permute-start | bytes 1769480 | tf_op jit(solution)/shard_map/ppermute | solution.py:16
  17.1 3.4 %collective-permute-start.5 = (bf16[256,1152]{1,0:T(8,128)(2,1)}, bf16[256,1152]{1,0:T(8,128)(2,1)S(1)}, u32[]{:S(2)}, u32[]{:S(2)}) collective-permute-start(bf16[256,1152]{1,0:T(8,128)(2,1)} %txt_ref.3), channel_id=1, source_target_pairs={{0,496},{16,0},{32,16},{48,32},{64,48},{80,64},{96,80},{112,96},{1... | collective-permute-start | bytes 1769480 | tf_op jit(solution)/shard_map/ppermute | solution.py:16
  20.5 1.9 %collective-permute-start.6 = (bf16[256,1152]{1,0:T(8,128)(2,1)}, bf16[256,1152]{1,0:T(8,128)(2,1)S(1)}, u32[]{:S(2)}, u32[]{:S(2)}) collective-permute-start(bf16[256,1152]{1,0:T(8,128)(2,1)} %img_ref.3), channel_id=1, source_target_pairs={{0,16},{16,32},{32,48},{48,64},{64,80},{80,96},{96,112},{112,128},... | collective-permute-start | bytes 1769480 | tf_op jit(solution)/shard_map/ppermute | solution.py:16
  23.7 1.1 copy-done.2
  24.8 1.1 copy-done.4
  25.8 1.6 %own_tile.1 = (bf16[256,1152]{1,0:T(8,128)(2,1)S(1)}, bf16[256,1152]{1,0:T(8,128)(2,1)S(1)}, f32[256,1152]{1,0:T(8,128)S(1)}, f32[256,1152]{1,0:T(8,128)S(1)}, f32[24,128]{1,0:T(8,128)S(1)}) custom-call(f32[1,1]{1,0:T(1,128)} %bitcast.6.temp_ref, f32[1,1]{1,0:T(1,128)} %bitcast.14.bias_ref, bf16[256,1152]{1,0:T(8,128)(2,1)S(1)} %copy-done.2, ...), custom_call_target="tpu_custom_call" | custom-call | tf_op jit(solution)/shard_map/own_tile/pallas_call | solution.py:80
  29.4 2.1 %pair.6 = (f32[256,1152]{1,0:T(8,128)S(1)}, f32[256,1152]{1,0:T(8,128)S(1)}, f32[24,128]{1,0:T(8,128)S(1)}, bf16[256,1152]{1,0:T(8,128)(2,1)S(1)}) custom-call(f32[1,1]{1,0:T(1,128)} %bitcast.7.refs_0_, f32[1,1]{1,0:T(1,128)} %bitcast.15.refs_1_, ...), custom_call_target="tpu_custom_call", output_to_operand_aliasing={{0}: (6, {}), {1}: (7, {}), {2}: (8, {})} | custom-call | flops 1000000000 | bytes 8388608 | tf_op jit(solution)/shard_map/pair/pallas_call | solution.py:138
  31.5 7.9 %collective-permute-start.4 = (bf16[256,1152]{1,0:T(8,128)(2,1)S(1)}, bf16[256,1152]{1,0:T(8,128)(2,1)}, u32[]{:S(2)}, u32[]{:S(2)}) collective-permute-start(bf16[256,1152]{1,0:T(8,128)(2,1)S(1)} %collective-permute-done.3.refs_5_), channel_id=1, source_target_pairs={{0,496},{16,0},{32,16},{48,32},{64,48},{80,64},{96,80},{112,96},{1... | collective-permute-start | bytes 1769480 | tf_op jit(solution)/shard_map/ppermute | solution.py:16
  39.4 1.9 %collective-permute-start.1 = (bf16[256,1152]{1,0:T(8,128)(2,1)S(1)}, bf16[256,1152]{1,0:T(8,128)(2,1)}, u32[]{:S(2)}, u32[]{:S(2)}) collective-permute-start(bf16[256,1152]{1,0:T(8,128)(2,1)S(1)} %collective-permute-done.refs_4_), channel_id=1, source_target_pairs={{0,16},{16,32},{32,48},{48,64},{64,80},{80,96},{96,112},{112,128},... | collective-permute-start | bytes 1769480 | tf_op jit(solution)/shard_map/ppermute | solution.py:16
  42.0 2.1 %pair.7 = (f32[256,1152]{1,0:T(8,128)S(1)}, f32[256,1152]{1,0:T(8,128)S(1)}, f32[24,128]{1,0:T(8,128)S(1)}, bf16[256,1152]{1,0:T(8,128)(2,1)S(1)}) custom-call(f32[1,1]{1,0:T(1,128)} %bitcast.8.refs_0_, f32[1,1]{1,0:T(1,128)} %bitcast.16.refs_1_, ...), custom_call_target="tpu_custom_call", output_to_operand_aliasing={{0}: (6, {}), {1}: (7, {}), {2}: (8, {})} | custom-call | flops 1000000000 | bytes 8388608 | tf_op jit(solution)/shard_map/pair/pallas_call | solution.py:138
  44.2 1.9 %collective-permute-start.9 = (bf16[256,1152]{1,0:T(8,128)(2,1)S(1)}, bf16[256,1152]{1,0:T(8,128)(2,1)}, u32[]{:S(2)}, u32[]{:S(2)}) collective-permute-start(bf16[256,1152]{1,0:T(8,128)(2,1)S(1)} %collective-permute-done.6.refs_5_), channel_id=1, source_target_pairs={{0,16},{16,32},{32,48},{48,64},{64,80},{80,96},{96,112},{112,128},... | collective-permute-start | bytes 1769480 | tf_op jit(solution)/shard_map/ppermute | solution.py:16
  46.1 7.9 %collective-permute-start.8 = (bf16[256,1152]{1,0:T(8,128)(2,1)S(1)}, bf16[256,1152]{1,0:T(8,128)(2,1)}, u32[]{:S(2)}, u32[]{:S(2)}) collective-permute-start(bf16[256,1152]{1,0:T(8,128)(2,1)S(1)} %collective-permute-done.5.refs_4_), channel_id=1, source_target_pairs={{0,496},{16,0},{32,16},{48,32},{64,48},{80,64},{96,80},{112,96},{1... | collective-permute-start | bytes 1769480 | tf_op jit(solution)/shard_map/ppermute | solution.py:16
  54.6 2.6 %collective-permute-done.1.refs_4_ = bf16[256,1152]{1,0:T(8,128)(2,1)} collective-permute-done((bf16[256,1152]{1,0:T(8,128)(2,1)S(1)}, bf16[256,1152]{1,0:T(8,128)(2,1)}, u32[]{:S(2)}, u32[]{:S(2)}) %collective-permute-start.1) | collective-permute-done | bytes 589856 | tf_op jit(solution)/shard_map/ppermute | solution.py:16
  57.2 3.9 %pair.8 = (f32[256,1152]{1,0:T(8,128)S(1)}, f32[256,1152]{1,0:T(8,128)S(1)}, f32[24,128]{1,0:T(8,128)S(1)}) custom-call(f32[1,1]{1,0:T(1,128)} %bitcast.9.refs_0_, f32[1,1]{1,0:T(1,128)} %bitcast.17.refs_1_, bf16[256,1152]{1,0:T(8,128)(2,1)S(1)} %get-tuple-element.51.refs_2_.img_n_ref, ...), custom_call_target="tpu_custom_call", output_to_operand_aliasing={{0}: (6, {}), {1}: (7, {}), {2}: (9, {})} | custom-call | flops 1000000000 | bytes 8388608 | tf_op jit(solution)/shard_map/pair/pallas_call | solution.py:138
  61.1 5.5 %collective-permute-start.7 = (bf16[256,1152]{1,0:T(8,128)(2,1)}, bf16[256,1152]{1,0:T(8,128)(2,1)}, u32[]{:S(2)}, u32[]{:S(2)}) collective-permute-start(bf16[256,1152]{1,0:T(8,128)(2,1)} %collective-permute-done.4.refs_5_), channel_id=1, source_target_pairs={{0,496},{16,0},{32,16},{48,32},{64,48},{80,64},{96,80},{112,96},{1... | collective-permute-start | bytes 1769480 | tf_op jit(solution)/shard_map/ppermute | solution.py:16
  66.6 1.9 %collective-permute-start.2 = (bf16[256,1152]{1,0:T(8,128)(2,1)}, bf16[256,1152]{1,0:T(8,128)(2,1)}, u32[]{:S(2)}, u32[]{:S(2)}) collective-permute-start(bf16[256,1152]{1,0:T(8,128)(2,1)} %collective-permute-done.1.refs_4_), channel_id=1, source_target_pairs={{0,16},{16,32},{32,48},{48,64},{64,80},{80,96},{96,112},{112,128},... | collective-permute-start | bytes 1769480 | tf_op jit(solution)/shard_map/ppermute | solution.py:16
  68.5 1.3 %collective-permute-done.9.refs_5_ = bf16[256,1152]{1,0:T(8,128)(2,1)} collective-permute-done((bf16[256,1152]{1,0:T(8,128)(2,1)S(1)}, bf16[256,1152]{1,0:T(8,128)(2,1)}, u32[]{:S(2)}, u32[]{:S(2)}) %collective-permute-start.9) | collective-permute-done | bytes 589856 | tf_op jit(solution)/shard_map/ppermute | solution.py:16
  69.8 3.5 %pair.9 = (f32[256,1152]{1,0:T(8,128)S(1)}, f32[256,1152]{1,0:T(8,128)S(1)}, f32[24,128]{1,0:T(8,128)S(1)}) custom-call(f32[1,1]{1,0:T(1,128)} %bitcast.10.refs_0_, f32[1,1]{1,0:T(1,128)} %bitcast.18.refs_1_, bf16[256,1152]{1,0:T(8,128)(2,1)S(1)} %get-tuple-element.51.refs_2_.img_n_ref, ...), custom_call_target="tpu_custom_call", output_to_operand_aliasing={{0}: (6, {}), {1}: (7, {}), {2}: (9, {})} | custom-call | flops 1000000000 | bytes 8388608 | tf_op jit(solution)/shard_map/pair/pallas_call | solution.py:138
  73.4 1.9 %collective-permute-start.10 = (bf16[256,1152]{1,0:T(8,128)(2,1)}, bf16[256,1152]{1,0:T(8,128)(2,1)}, u32[]{:S(2)}, u32[]{:S(2)}) collective-permute-start(bf16[256,1152]{1,0:T(8,128)(2,1)} %collective-permute-done.9.refs_5_), channel_id=1, source_target_pairs={{0,16},{16,32},{32,48},{48,64},{64,80},{80,96},{96,112},{112,128},... | collective-permute-start | bytes 1769480 | tf_op jit(solution)/shard_map/ppermute | solution.py:16
  75.3 7.3 %collective-permute-start.11 = (bf16[256,1152]{1,0:T(8,128)(2,1)}, bf16[256,1152]{1,0:T(8,128)(2,1)}, u32[]{:S(2)}, u32[]{:S(2)}) collective-permute-start(bf16[256,1152]{1,0:T(8,128)(2,1)} %collective-permute-done.8.refs_4_), channel_id=1, source_target_pairs={{0,496},{16,0},{32,16},{48,32},{64,48},{80,64},{96,80},{112,96},{1... | collective-permute-start | bytes 1769480 | tf_op jit(solution)/shard_map/ppermute | solution.py:16
  83.3 11.9 %all-to-all-start = ((f32[16,24,128]{2,1,0:T(8,128)}), f32[16,24,128]{2,1,0:T(8,128)}, u32[]{:S(2)}, u32[]{:S(2)}) async-start(f32[16,24,128]{2,1,0:T(8,128)} %copy-done.1), calls=%async_computation | async-start | bytes 393216 | tf_op jit(solution)/shard_map/all_to_all | solution.py:203
  95.2 1.9 %collective-permute-start.13 = (bf16[256,1152]{1,0:T(8,128)(2,1)}, bf16[256,1152]{1,0:T(8,128)(2,1)}, u32[]{:S(2)}, u32[]{:S(2)}) collective-permute-start(bf16[256,1152]{1,0:T(8,128)(2,1)} %collective-permute-done.7.refs_5_), channel_id=1, source_target_pairs={{0,496},{16,0},{32,16},{48,32},{64,48},{80,64},{96,80},{112,96},{1... | collective-permute-start | bytes 1769480 | tf_op jit(solution)/shard_map/ppermute | solution.py:16
  97.2 3.4 %collective-permute-start.12 = (bf16[256,1152]{1,0:T(8,128)(2,1)}, bf16[256,1152]{1,0:T(8,128)(2,1)}, u32[]{:S(2)}, u32[]{:S(2)}) collective-permute-start(bf16[256,1152]{1,0:T(8,128)(2,1)} %collective-permute-done.2.refs_4_), channel_id=1, source_target_pairs={{0,16},{16,32},{32,48},{48,64},{64,80},{80,96},{96,112},{112,128},... | collective-permute-start | bytes 1769480 | tf_op jit(solution)/shard_map/ppermute | solution.py:16
  100.5 3.2 %pair.10 = (f32[256,1152]{1,0:T(8,128)S(1)}, f32[256,1152]{1,0:T(8,128)S(1)}) custom-call(f32[1,1]{1,0:T(1,128)} %bitcast.11.refs_0_, f32[1,1]{1,0:T(1,128)} %bitcast.19.refs_1_, bf16[256,1152]{1,0:T(8,128)(2,1)S(1)} %get-tuple-element.51.refs_2_.img_n_ref, ...), custom_call_target="tpu_custom_call", output_to_operand_aliasing={{0}: (6, {}), {1}: (7, {})} | custom-call | flops 1000000000 | bytes 8388608 | tf_op jit(solution)/shard_map/pair/pallas_call | solution.py:138
  103.7 2.2 %all-to-all-done.parts_ref = f32[16,24,128]{2,1,0:T(8,128)} async-done(((f32[16,24,128]{2,1,0:T(8,128)}), f32[16,24,128]{2,1,0:T(8,128)}, u32[]{:S(2)}, u32[]{:S(2)}) %all-to-all-start) | async-done | bytes 196640 | tf_op jit(solution)/shard_map/all_to_all | solution.py:203
  107.6 5.8 %all-to-all-start.1 = ((f32[32,24,128]{2,1,0:T(8,128)}), f32[32,24,128]{2,1,0:T(8,128)}, u32[]{:S(2)}, u32[]{:S(2)}) async-start(f32[32,24,128]{2,1,0:T(8,128)} %copy-done), calls=%async_computation.1 | async-start | bytes 786432 | tf_op jit(solution)/shard_map/all_to_all | solution.py:203
  113.4 3.3 %pair.11 = (f32[256,1152]{1,0:T(8,128)S(1)}, f32[256,1152]{1,0:T(8,128)S(1)}) custom-call(f32[1,1]{1,0:T(1,128)} %bitcast.12.refs_0_, f32[1,1]{1,0:T(1,128)} %bitcast.20.refs_1_, bf16[256,1152]{1,0:T(8,128)(2,1)S(1)} %get-tuple-element.51.refs_2_.img_n_ref, ...), custom_call_target="tpu_custom_call", output_to_operand_aliasing={{0}: (6, {}), {1}: (7, {})} | custom-call | flops 1000000000 | bytes 8388608 | tf_op jit(solution)/shard_map/pair/pallas_call | solution.py:138
  116.7 4.5 %collective-permute-done.12.t_ref = bf16[256,1152]{1,0:T(8,128)(2,1)} collective-permute-done((bf16[256,1152]{1,0:T(8,128)(2,1)}, bf16[256,1152]{1,0:T(8,128)(2,1)}, u32[]{:S(2)}, u32[]{:S(2)}) %collective-permute-start.12) | collective-permute-done | bytes 589856 | tf_op jit(solution)/shard_map/ppermute | solution.py:16
  121.3 4.8 %last.1 = (f32[256,1152]{1,0:T(8,128)}, f32[256,1152]{1,0:T(8,128)}) custom-call(f32[1,1]{1,0:T(1,128)} %bitcast.13.temp_ref, f32[1,1]{1,0:T(1,128)} %bitcast.21.bias_ref, bf16[256,1152]{1,0:T(8,128)(2,1)S(1)} %get-tuple-element.51.refs_2_.img_n_ref, bf16[256,1152]{1,0:T(8,128)(2,1)S(1)} %get-tuple-element.52.refs_3_.txt_n_ref, ...), custom_call_target="tpu_custom_call" | custom-call | flops 2000000000 | bytes 8388608 | tf_op jit(solution)/shard_map/last/pallas_call | solution.py:163
  126.1 1.9 %all-to-all-done.1.parts_ref = f32[32,24,128]{2,1,0:T(8,128)} async-done(((f32[32,24,128]{2,1,0:T(8,128)}), f32[32,24,128]{2,1,0:T(8,128)}, u32[]{:S(2)}, u32[]{:S(2)}) %all-to-all-start.1) | async-done | bytes 393248 | tf_op jit(solution)/shard_map/all_to_all | solution.py:203
  128.1 1.7 %finish.1 = (f32[1,1]{1,0:T(1,128)}, f32[1,1]{1,0:T(1,128)}, f32[1,1]{1,0:T(1,128)}) custom-call(f32[32,24,128]{2,1,0:T(8,128)} %all-to-all-done.1.parts_ref), custom_call_target="tpu_custom_call" | custom-call | flops 115000000512 | bytes 8388608 | tf_op jit(solution)/shard_map/finish/pallas_call | solution.py:192
  (23 shorter events, 5.7 us)
Async XLA Ops:
  0.6 27.8 %collective-permute-start = (bf16[256,1152]{1,0:T(8,128)(2,1)}, bf16[256,1152]{1,0:T(8,128)(2,1)S(1)}, u32[]{:S(2)}, u32[]{:S(2)}) collective-permute-start(bf16[256,1152]{1,0:T(8,128)(2,1)} %txt_ref.3), channel_id=1, source_target_pairs={{0,16},{16,32},{32,48},{48,64},{64,80},{80,96},{96,112},{112,128},... | collective-permute-start | bytes 1769480 | tf_op jit(solution)/shard_map/ppermute | solution.py:16
  5.5 23.9 %collective-permute-start.3 = (bf16[256,1152]{1,0:T(8,128)(2,1)}, bf16[256,1152]{1,0:T(8,128)(2,1)S(1)}, u32[]{:S(2)}, u32[]{:S(2)}) collective-permute-start(bf16[256,1152]{1,0:T(8,128)(2,1)} %img_ref.3), channel_id=1, source_target_pairs={{0,496},{16,0},{32,16},{48,32},{64,48},{80,64},{96,80},{112,96},{1... | collective-permute-start | bytes 1769480 | tf_op jit(solution)/shard_map/ppermute | solution.py:16
  17.1 24.9 %collective-permute-start.5 = (bf16[256,1152]{1,0:T(8,128)(2,1)}, bf16[256,1152]{1,0:T(8,128)(2,1)S(1)}, u32[]{:S(2)}, u32[]{:S(2)}) collective-permute-start(bf16[256,1152]{1,0:T(8,128)(2,1)} %txt_ref.3), channel_id=1, source_target_pairs={{0,496},{16,0},{32,16},{48,32},{64,48},{80,64},{96,80},{112,96},{1... | collective-permute-start | bytes 1769480 | tf_op jit(solution)/shard_map/ppermute | solution.py:16
  20.5 21.6 %collective-permute-start.6 = (bf16[256,1152]{1,0:T(8,128)(2,1)}, bf16[256,1152]{1,0:T(8,128)(2,1)S(1)}, u32[]{:S(2)}, u32[]{:S(2)}) collective-permute-start(bf16[256,1152]{1,0:T(8,128)(2,1)} %img_ref.3), channel_id=1, source_target_pairs={{0,16},{16,32},{32,48},{48,64},{64,80},{80,96},{96,112},{112,128},... | collective-permute-start | bytes 1769480 | tf_op jit(solution)/shard_map/ppermute | solution.py:16
  23.7 1.1 copy-start.2
  24.8 1.1 copy-start.4
  31.5 23.1 %collective-permute-start.4 = (bf16[256,1152]{1,0:T(8,128)(2,1)S(1)}, bf16[256,1152]{1,0:T(8,128)(2,1)}, u32[]{:S(2)}, u32[]{:S(2)}) collective-permute-start(bf16[256,1152]{1,0:T(8,128)(2,1)S(1)} %collective-permute-done.3.refs_5_), channel_id=1, source_target_pairs={{0,496},{16,0},{32,16},{48,32},{64,48},{80,64},{96,80},{112,96},{1... | collective-permute-start | bytes 1769480 | tf_op jit(solution)/shard_map/ppermute | solution.py:16
  39.4 17.8 %collective-permute-start.1 = (bf16[256,1152]{1,0:T(8,128)(2,1)S(1)}, bf16[256,1152]{1,0:T(8,128)(2,1)}, u32[]{:S(2)}, u32[]{:S(2)}) collective-permute-start(bf16[256,1152]{1,0:T(8,128)(2,1)S(1)} %collective-permute-done.refs_4_), channel_id=1, source_target_pairs={{0,16},{16,32},{32,48},{48,64},{64,80},{80,96},{96,112},{112,128},... | collective-permute-start | bytes 1769480 | tf_op jit(solution)/shard_map/ppermute | solution.py:16
  44.2 25.7 %collective-permute-start.9 = (bf16[256,1152]{1,0:T(8,128)(2,1)S(1)}, bf16[256,1152]{1,0:T(8,128)(2,1)}, u32[]{:S(2)}, u32[]{:S(2)}) collective-permute-start(bf16[256,1152]{1,0:T(8,128)(2,1)S(1)} %collective-permute-done.6.refs_5_), channel_id=1, source_target_pairs={{0,16},{16,32},{32,48},{48,64},{64,80},{80,96},{96,112},{112,128},... | collective-permute-start | bytes 1769480 | tf_op jit(solution)/shard_map/ppermute | solution.py:16
  46.1 23.7 %collective-permute-start.8 = (bf16[256,1152]{1,0:T(8,128)(2,1)S(1)}, bf16[256,1152]{1,0:T(8,128)(2,1)}, u32[]{:S(2)}, u32[]{:S(2)}) collective-permute-start(bf16[256,1152]{1,0:T(8,128)(2,1)S(1)} %collective-permute-done.5.refs_4_), channel_id=1, source_target_pairs={{0,496},{16,0},{32,16},{48,32},{64,48},{80,64},{96,80},{112,96},{1... | collective-permute-start | bytes 1769480 | tf_op jit(solution)/shard_map/ppermute | solution.py:16
  61.1 34.2 %collective-permute-start.7 = (bf16[256,1152]{1,0:T(8,128)(2,1)}, bf16[256,1152]{1,0:T(8,128)(2,1)}, u32[]{:S(2)}, u32[]{:S(2)}) collective-permute-start(bf16[256,1152]{1,0:T(8,128)(2,1)} %collective-permute-done.4.refs_5_), channel_id=1, source_target_pairs={{0,496},{16,0},{32,16},{48,32},{64,48},{80,64},{96,80},{112,96},{1... | collective-permute-start | bytes 1769480 | tf_op jit(solution)/shard_map/ppermute | solution.py:16
  66.6 30.6 %collective-permute-start.2 = (bf16[256,1152]{1,0:T(8,128)(2,1)}, bf16[256,1152]{1,0:T(8,128)(2,1)}, u32[]{:S(2)}, u32[]{:S(2)}) collective-permute-start(bf16[256,1152]{1,0:T(8,128)(2,1)} %collective-permute-done.1.refs_4_), channel_id=1, source_target_pairs={{0,16},{16,32},{32,48},{48,64},{64,80},{80,96},{96,112},{112,128},... | collective-permute-start | bytes 1769480 | tf_op jit(solution)/shard_map/ppermute | solution.py:16
  73.4 32.5 %collective-permute-start.10 = (bf16[256,1152]{1,0:T(8,128)(2,1)}, bf16[256,1152]{1,0:T(8,128)(2,1)}, u32[]{:S(2)}, u32[]{:S(2)}) collective-permute-start(bf16[256,1152]{1,0:T(8,128)(2,1)} %collective-permute-done.9.refs_5_), channel_id=1, source_target_pairs={{0,16},{16,32},{32,48},{48,64},{64,80},{80,96},{96,112},{112,128},... | collective-permute-start | bytes 1769480 | tf_op jit(solution)/shard_map/ppermute | solution.py:16
  75.3 30.6 %collective-permute-start.11 = (bf16[256,1152]{1,0:T(8,128)(2,1)}, bf16[256,1152]{1,0:T(8,128)(2,1)}, u32[]{:S(2)}, u32[]{:S(2)}) collective-permute-start(bf16[256,1152]{1,0:T(8,128)(2,1)} %collective-permute-done.8.refs_4_), channel_id=1, source_target_pairs={{0,496},{16,0},{32,16},{48,32},{64,48},{80,64},{96,80},{112,96},{1... | collective-permute-start | bytes 1769480 | tf_op jit(solution)/shard_map/ppermute | solution.py:16
  82.6 0.7 copy-start.1
  83.3 22.6 %all-to-all-start = ((f32[16,24,128]{2,1,0:T(8,128)}), f32[16,24,128]{2,1,0:T(8,128)}, u32[]{:S(2)}, u32[]{:S(2)}) async-start(f32[16,24,128]{2,1,0:T(8,128)} %copy-done.1), calls=%async_computation | async-start | bytes 393216 | tf_op jit(solution)/shard_map/all_to_all | solution.py:203
  95.2 21.5 %collective-permute-start.13 = (bf16[256,1152]{1,0:T(8,128)(2,1)}, bf16[256,1152]{1,0:T(8,128)(2,1)}, u32[]{:S(2)}, u32[]{:S(2)}) collective-permute-start(bf16[256,1152]{1,0:T(8,128)(2,1)} %collective-permute-done.7.refs_5_), channel_id=1, source_target_pairs={{0,496},{16,0},{32,16},{48,32},{64,48},{80,64},{96,80},{112,96},{1... | collective-permute-start | bytes 1769480 | tf_op jit(solution)/shard_map/ppermute | solution.py:16
  97.2 24.1 %collective-permute-start.12 = (bf16[256,1152]{1,0:T(8,128)(2,1)}, bf16[256,1152]{1,0:T(8,128)(2,1)}, u32[]{:S(2)}, u32[]{:S(2)}) collective-permute-start(bf16[256,1152]{1,0:T(8,128)(2,1)} %collective-permute-done.2.refs_4_), channel_id=1, source_target_pairs={{0,16},{16,32},{32,48},{48,64},{64,80},{80,96},{96,112},{112,128},... | collective-permute-start | bytes 1769480 | tf_op jit(solution)/shard_map/ppermute | solution.py:16
  106.9 0.7 copy-start
  107.6 20.4 %all-to-all-start.1 = ((f32[32,24,128]{2,1,0:T(8,128)}), f32[32,24,128]{2,1,0:T(8,128)}, u32[]{:S(2)}, u32[]{:S(2)}) async-start(f32[32,24,128]{2,1,0:T(8,128)} %copy-done), calls=%async_computation.1 | async-start | bytes 786432 | tf_op jit(solution)/shard_map/all_to_all | solution.py:203
  113.4 7.9 %copy-start.3 = (bf16[256,1152]{1,0:T(8,128)(2,1)S(1)}, bf16[256,1152]{1,0:T(8,128)(2,1)}, u32[]{:S(2)}) copy-start(bf16[256,1152]{1,0:T(8,128)(2,1)} %img_ref.3) | copy-start | bytes 1769476
  113.4 7.9 %copy-start.5 = (bf16[256,1152]{1,0:T(8,128)(2,1)S(1)}, bf16[256,1152]{1,0:T(8,128)(2,1)}, u32[]{:S(2)}) copy-start(bf16[256,1152]{1,0:T(8,128)(2,1)} %txt_ref.3) | copy-start | bytes 1769476
